TPU v7x, 128 devices: a whole 4x4x4 slice. The times are simulated.
128 devices in a mesh: row: 16 (over x, z_lo, core), col: 8 (over y, z_hi).
Axes of the slice: x: 4, y: 4, z: 4 (z_hi: 2, z_lo: 2; z = z_hi * 2 + z_lo), core: 2. Of those that a mesh axis runs over, the one named last changes fastest.
Arguments:
- features: bfloat16 [32768, 512], P(('row', 'col')), may hold values from -6 to 6
- weight: bfloat16 [512, 512], replicated, may hold values from -0.25 to 0.25
- cotangent: bfloat16 [32768, 512], P(('col', 'row')), may hold values from -6 to 6
- tiles: bfloat16 [16, 8, 128, 128, 128], P('row', 'col'), may hold values from -0.09375 to 0.09375
- tile_rows: int32 [16, 8, 128], P('row', 'col'), may hold values from 0 to 31, as said below
- tile_cols: int32 [16, 8, 128], P('row', 'col'), may hold values from 0 to 15
- tile_count: int32 [16, 8, 1], P('row', 'col'), may hold values from 16 to 128, as said below
Outputs:
- activations: bfloat16 [32768, 512], P(('col', 'row'))
- weight_grad: float32 [512, 512], replicated
- feature_grad: bfloat16 [32768, 512], P(('row', 'col'))
Inputs may be any that keep to these rules, and one draw needn't show every extreme that they name: Within one grid cell the live slots name distinct (tile_rows, tile_cols) pairs. `tile_count`: some grid cell holds 128 live tiles in every draw.
All inputs are finite; a program needn't handle non-finite values.
Results may differ from a plain program's by a relative error of at most 0.0065.
Values may be sent and summed in bfloat16 or wider, within the bound.
No kernel may reach another device: no remote copies, remote signals or barrier semaphores. Data moves between devices by JAX's collectives and lax.ppermute only.
A program may use at most 128 MiB of HBM per device.

v0:
```python
import math

import jax
import jax.numpy as jnp
from jax import lax
from jax.sharding import PartitionSpec as P


def silu_slope(values):
    sigma = jax.nn.sigmoid(values)
    return sigma * (1.0 + values * (1.0 - sigma))


def tile_pass(source, tile_set, pick_ids, place_ids, live_mask, out_blocks, forward):
    slots = tile_set.shape[0]
    side = tile_set.shape[-1]
    width = source.shape[-1]
    group = math.gcd(slots, 32)
    turns = slots // group
    items = (
        tile_set.reshape(turns, group, side, side),
        pick_ids.reshape(turns, group),
        place_ids.reshape(turns, group),
        live_mask.reshape(turns, group),
    )

    def one_group(running, item):
        group_tiles, group_pick, group_place, group_live = item
        picked = source[group_pick]
        if forward:
            product = jnp.einsum(
                "tpq,tqf->tpf", group_tiles, picked, preferred_element_type=jnp.float32
            )
        else:
            product = jnp.einsum(
                "tpq,tpf->tqf", group_tiles, picked, preferred_element_type=jnp.float32
            )
        weighted = product * group_live.astype(jnp.float32)[:, None, None]
        return (running.at[group_place].add(weighted), None)

    start = jnp.zeros((out_blocks, side, width), jnp.float32)
    result, _ = lax.scan(one_group, start, items)
    return result.reshape(out_blocks * side, width)


def local(features, weight, cotangent, tiles, tile_rows, tile_cols, tile_count):
    width = weight.shape[0]
    tile_set = tiles[0, 0]
    side = tile_set.shape[-1]
    row_ids = tile_rows[0, 0]
    col_ids = tile_cols[0, 0]
    live_mask = lax.iota(jnp.int32, tile_set.shape[0]) < tile_count[0, 0, 0]
    row_devs = lax.axis_size("row")
    col_devs = lax.axis_size("col")
    own_rows = features.shape[0]
    own_blocks = own_rows // side
    row_blocks = own_blocks * row_devs
    col_blocks = own_blocks * col_devs
    node_total = own_rows * row_devs * col_devs
    row_place = lax.axis_index("row")
    stripe = lax.all_gather(features, "col", axis=0, tiled=True).reshape(col_blocks, side, width)
    partial_value = tile_pass(stripe, tile_set, col_ids, row_ids, live_mask, row_blocks, True)
    summed = lax.psum(partial_value, "row")
    mixed_stripe = summed.astype(jnp.bfloat16)
    cot_stripe = lax.all_gather(cotangent, "row", axis=0, tiled=True)
    pre_stripe = jnp.dot(mixed_stripe, weight, preferred_element_type=jnp.float32)
    grad_stripe = (cot_stripe.astype(jnp.float32) * silu_slope(pre_stripe)).astype(jnp.bfloat16)
    grad_mixed = jnp.dot(grad_stripe, weight.T, preferred_element_type=jnp.float32).astype(
        jnp.bfloat16
    )
    offset = row_place * own_rows
    own_pre = lax.dynamic_slice_in_dim(pre_stripe, offset, own_rows, 0)
    activ_out = jax.nn.silu(own_pre).astype(jnp.bfloat16)
    own_mixed = lax.dynamic_slice_in_dim(mixed_stripe, offset, own_rows, 0)
    own_grad = lax.dynamic_slice_in_dim(grad_stripe, offset, own_rows, 0)
    local_wgrad = jnp.einsum("nf,ng->fg", own_mixed, own_grad, preferred_element_type=jnp.float32)
    weight_grad = lax.psum(local_wgrad, ("row", "col")) * float(node_total) ** (-0.5)
    grad_blocks = grad_mixed.reshape(row_blocks, side, width)
    back_partial = tile_pass(grad_blocks, tile_set, row_ids, col_ids, live_mask, col_blocks, False)
    feature_grad = lax.psum_scatter(back_partial, "col", scatter_dimension=0, tiled=True).astype(
        jnp.bfloat16
    )
    return (activ_out, weight_grad, feature_grad)


def solution(mesh):
    in_specs = (
        P(("row", "col"), None),
        P(),
        P(("col", "row"), None),
        P("row", "col", None, None, None),
        P("row", "col", None),
        P("row", "col", None),
        P("row", "col", None),
    )
    out_specs = (P(("col", "row"), None), P(), P(("row", "col"), None))
    return jax.shard_map(local, mesh=mesh, in_specs=in_specs, out_specs=out_specs, check_vma=False)
```

profile of v0, /device:TPU:17, one launch (start us, length us, event | category | flops | bytes accessed | tf_op | source)
XLA Modules:
  0.0 623.6 jit_solution(10653289790248903881)
XLA Ops:
  7.2 0.7 all-gather.3.cloned.1.call-update
  8.0 0.7 all-gather.5.cloned.1.call-update
  8.7 0.0 all-reduce.3.cloned.1.call-start
  8.7 0.5 broadcast.106
  9.2 1.3 reduce.6
  10.5 0.1 reshape_squeeze.12
  10.6 1.3 reduce.7
  12.0 0.1 reshape_squeeze.14
  12.7 6.4 %copy.10 = bf16[1,1,128,128,128]{3,4,2,1,0:T(8,128)(2,1)} copy(bf16[1,1,128,128,128]{4,3,2,1,0:T(8,128)(2,1)} %param.14) | data formatting | bytes 8388608 | tf_op args[3]
  19.1 45.7 %all-gather.3.cloned.1.call-done = bf16[2048,512]{1,0:T(8,128)(2,1)} async-done(((bf16[256,512]{1,0:T(8,128)(2,1)}), bf16[2048,512]{1,0:T(8,128)(2,1)}) %all-gather.3.cloned.1.call-update) | async-done | bytes 2097168 | tf_op jit(solution)/shard_map/all_gather | solution.py:61
  64.8 4.3 broadcast_in_dim.4
  69.1 114.0 %while.20 = (s32[]{:T(128)}, f32[32,128,512]{2,1,0:T(8,128)}, s32[4,32]{1,0:T(4,128)S(1)}, bf16[4,32,128,128]{3,2,1,0:T(8,128)(2,1)}, s32[4,32]{1,0:T(4,128)S(1)...) while((s32[]{:T(128)}, f32[32,128,512]{2,1,0:T(8,128)}, ...), condition=%wide.region_2.3_spmd, body=%wide.region_0.2_spmd.sunk | while | flops 541066496 | bytes 47191804 | solution.py:42
  69.1 2.8 gather_fusion
  71.9 7.0 %broadcast_multiply_fusion.5 = f32[32,128,512]{2,1,0:T(8,128)} fusion(f32[32]{0:T(128)S(1)} %fusion.37, bf16[32,128,512]{2,1,0:T(8,128)(2,1)} %gather_fusion, bf16[4,32,128,128]{3,2,1,0:T(8,128)(2,1)} %get-tuple-element.233, s32[]{:T(128)} %get-tuple-element.222), kind=kOutput, calls=%fused_computation.4.clone.1 | convolution fusion | flops 538968064 | bytes 13632128 | tf_op jit(solution)/shard_map/while/body/eval_jaxpr/tpq,tqf->tpf/dot_general | solution.py:31
  78.9 19.0 %scatter_fusion = f32[32,128,512]{2,1,0:T(8,128)} fusion(f32[32,128,512]{2,1,0:T(8,128)} %get-tuple-element.223, s32[32]{0:T(128)S(1)} %get-tuple-element.203, f32[32,128,512]{2,1,0:T(8,128)} %broadcast_multiply_fusion.5), kind=kCustom, calls=%fused_computation.2.clone.1 | custom fusion | flops 2097152 | bytes 25165952 | tf_op jit(solution)/shard_map/while/body/eval_jaxpr/scatter-add | solution.py:39
  97.9 2.8 gather_fusion
  100.7 7.0 %broadcast_multiply_fusion.5 = f32[32,128,512]{2,1,0:T(8,128)} fusion(f32[32]{0:T(128)S(1)} %fusion.37, bf16[32,128,512]{2,1,0:T(8,128)(2,1)} %gather_fusion, bf16[4,32,128,128]{3,2,1,0:T(8,128)(2,1)} %get-tuple-element.233, s32[]{:T(128)} %get-tuple-element.222), kind=kOutput, calls=%fused_computation.4.clone.1 | convolution fusion | flops 538968064 | bytes 13632128 | tf_op jit(solution)/shard_map/while/body/eval_jaxpr/tpq,tqf->tpf/dot_general | solution.py:31
  107.7 19.0 %scatter_fusion = f32[32,128,512]{2,1,0:T(8,128)} fusion(f32[32,128,512]{2,1,0:T(8,128)} %get-tuple-element.223, s32[32]{0:T(128)S(1)} %get-tuple-element.203, f32[32,128,512]{2,1,0:T(8,128)} %broadcast_multiply_fusion.5), kind=kCustom, calls=%fused_computation.2.clone.1 | custom fusion | flops 2097152 | bytes 25165952 | tf_op jit(solution)/shard_map/while/body/eval_jaxpr/scatter-add | solution.py:39
  126.7 2.8 gather_fusion
  129.5 7.0 %broadcast_multiply_fusion.5 = f32[32,128,512]{2,1,0:T(8,128)} fusion(f32[32]{0:T(128)S(1)} %fusion.37, bf16[32,128,512]{2,1,0:T(8,128)(2,1)} %gather_fusion, bf16[4,32,128,128]{3,2,1,0:T(8,128)(2,1)} %get-tuple-element.233, s32[]{:T(128)} %get-tuple-element.222), kind=kOutput, calls=%fused_computation.4.clone.1 | convolution fusion | flops 538968064 | bytes 13632128 | tf_op jit(solution)/shard_map/while/body/eval_jaxpr/tpq,tqf->tpf/dot_general | solution.py:31
  136.5 18.2 %scatter_fusion = f32[32,128,512]{2,1,0:T(8,128)} fusion(f32[32,128,512]{2,1,0:T(8,128)} %get-tuple-element.223, s32[32]{0:T(128)S(1)} %get-tuple-element.203, f32[32,128,512]{2,1,0:T(8,128)} %broadcast_multiply_fusion.5), kind=kCustom, calls=%fused_computation.2.clone.1 | custom fusion | flops 2097152 | bytes 25165952 | tf_op jit(solution)/shard_map/while/body/eval_jaxpr/scatter-add | solution.py:39
  154.7 2.8 gather_fusion
  157.5 7.0 %broadcast_multiply_fusion.5 = f32[32,128,512]{2,1,0:T(8,128)} fusion(f32[32]{0:T(128)S(1)} %fusion.37, bf16[32,128,512]{2,1,0:T(8,128)(2,1)} %gather_fusion, bf16[4,32,128,128]{3,2,1,0:T(8,128)(2,1)} %get-tuple-element.233, s32[]{:T(128)} %get-tuple-element.222), kind=kOutput, calls=%fused_computation.4.clone.1 | convolution fusion | flops 538968064 | bytes 13632128 | tf_op jit(solution)/shard_map/while/body/eval_jaxpr/tpq,tqf->tpf/dot_general | solution.py:31
  164.5 18.6 %scatter_fusion = f32[32,128,512]{2,1,0:T(8,128)} fusion(f32[32,128,512]{2,1,0:T(8,128)} %get-tuple-element.223, s32[32]{0:T(128)S(1)} %get-tuple-element.203, f32[32,128,512]{2,1,0:T(8,128)} %broadcast_multiply_fusion.5), kind=kCustom, calls=%fused_computation.2.clone.1 | custom fusion | flops 2097152 | bytes 25165952 | tf_op jit(solution)/shard_map/while/body/eval_jaxpr/scatter-add | solution.py:39
  183.1 182.5 %all-reduce.4 = bf16[4096,512]{1,0:T(8,128)(2,1)} all-reduce(f32[4096,512]{1,0:T(8,128)} %bitcast.77), channel_id=1, replica_groups=mesh['row'=16,'col'=8] {'row'}, use_global_device_ids=true, to_apply=%region_3.4 | all-reduce | flops 2097152 | bytes 12582912 | tf_op jit(solution)/shard_map/psum | solution.py:63
  365.5 8.6 %multiply_convert_fusion = (bf16[4096,512]{1,0:T(8,128)(2,1)S(1)}, f32[4096,512]{1,0:T(8,128)}) fusion(bf16[4096,512]{1,0:T(8,128)(2,1)} %all-gather.5.cloned.1.call-done, bf16[4096,512]{1,0:T(8,128)(2,1)} %all-reduce.4, bf16[512,512]{1,0:T(8,128)(2,1)S(1)} %copy-done), kind=kOutput, calls=%fused_computation.34 | convolution fusion | flops 2168455168 | bytes 21495808 | tf_op jit(solution)/shard_map/dot_general | solution.py:66
  374.1 4.3 convolution_convert_fusion
  378.5 2.2 fusion.16
  380.7 0.2 reduce-scatter.2.cloned.1.call-start
  381.0 2.5 broadcast_in_dim.8
  383.5 121.7 %while.21 = (s32[]{:T(128)}, f32[16,128,512]{2,1,0:T(8,128)}, s32[4,32]{1,0:T(4,128)S(1)}, bf16[4,32,128,128]{2,3,1,0:T(8,128)(2,1)}, s32[4,32]{1,0:T(4,128)S(1)...) while((s32[]{:T(128)}, f32[16,128,512]{2,1,0:T(8,128)}, s32[4,32]{1,0:T(4,128)S(1)}, ...), condition=%wide.region_7.8_spmd, body=%wide.region_5.7_spmd.sunk | while | flops 541066496 | bytes 47191804 | solution.py:42
  383.5 4.9 gather_fusion.1
  388.4 7.0 %broadcast_multiply_fusion.6 = f32[32,128,512]{2,1,0:T(8,128)} fusion(f32[32]{0:T(128)S(1)} %fusion.41, bf16[32,128,512]{2,1,0:T(8,128)(2,1)} %gather_fusion.1, bf16[4,32,128,128]{2,3,1,0:T(8,128)(2,1)} %get-tuple-element.257, s32[]{:T(128)} %get-tuple-element.246), kind=kOutput, calls=%fused_computation.19.clone.1 | convolution fusion | flops 538968064 | bytes 13632128 | tf_op jit(solution)/shard_map/while/body/eval_jaxpr/tpq,tpf->tqf/dot_general | solution.py:35
  395.4 18.4 %scatter_fusion.1 = f32[16,128,512]{2,1,0:T(8,128)} fusion(f32[16,128,512]{2,1,0:T(8,128)} %get-tuple-element.247, s32[32]{0:T(128)S(1)} %get-tuple-element.212, f32[32,128,512]{2,1,0:T(8,128)} %broadcast_multiply_fusion.6), kind=kCustom, calls=%fused_computation.3.clone.1 | custom fusion | flops 2097152 | bytes 25165952 | tf_op jit(solution)/shard_map/while/body/eval_jaxpr/scatter-add | solution.py:39
  413.8 5.0 gather_fusion.1
  418.8 7.0 %broadcast_multiply_fusion.6 = f32[32,128,512]{2,1,0:T(8,128)} fusion(f32[32]{0:T(128)S(1)} %fusion.41, bf16[32,128,512]{2,1,0:T(8,128)(2,1)} %gather_fusion.1, bf16[4,32,128,128]{2,3,1,0:T(8,128)(2,1)} %get-tuple-element.257, s32[]{:T(128)} %get-tuple-element.246), kind=kOutput, calls=%fused_computation.19.clone.1 | convolution fusion | flops 538968064 | bytes 13632128 | tf_op jit(solution)/shard_map/while/body/eval_jaxpr/tpq,tpf->tqf/dot_general | solution.py:35
  425.7 18.4 %scatter_fusion.1 = f32[16,128,512]{2,1,0:T(8,128)} fusion(f32[16,128,512]{2,1,0:T(8,128)} %get-tuple-element.247, s32[32]{0:T(128)S(1)} %get-tuple-element.212, f32[32,128,512]{2,1,0:T(8,128)} %broadcast_multiply_fusion.6), kind=kCustom, calls=%fused_computation.3.clone.1 | custom fusion | flops 2097152 | bytes 25165952 | tf_op jit(solution)/shard_map/while/body/eval_jaxpr/scatter-add | solution.py:39
  444.1 5.0 gather_fusion.1
  449.1 7.0 %broadcast_multiply_fusion.6 = f32[32,128,512]{2,1,0:T(8,128)} fusion(f32[32]{0:T(128)S(1)} %fusion.41, bf16[32,128,512]{2,1,0:T(8,128)(2,1)} %gather_fusion.1, bf16[4,32,128,128]{2,3,1,0:T(8,128)(2,1)} %get-tuple-element.257, s32[]{:T(128)} %get-tuple-element.246), kind=kOutput, calls=%fused_computation.19.clone.1 | convolution fusion | flops 538968064 | bytes 13632128 | tf_op jit(solution)/shard_map/while/body/eval_jaxpr/tpq,tpf->tqf/dot_general | solution.py:35
  456.0 18.6 %scatter_fusion.1 = f32[16,128,512]{2,1,0:T(8,128)} fusion(f32[16,128,512]{2,1,0:T(8,128)} %get-tuple-element.247, s32[32]{0:T(128)S(1)} %get-tuple-element.212, f32[32,128,512]{2,1,0:T(8,128)} %broadcast_multiply_fusion.6), kind=kCustom, calls=%fused_computation.3.clone.1 | custom fusion | flops 2097152 | bytes 25165952 | tf_op jit(solution)/shard_map/while/body/eval_jaxpr/scatter-add | solution.py:39
  474.6 4.9 gather_fusion.1
  479.6 7.0 %broadcast_multiply_fusion.6 = f32[32,128,512]{2,1,0:T(8,128)} fusion(f32[32]{0:T(128)S(1)} %fusion.41, bf16[32,128,512]{2,1,0:T(8,128)(2,1)} %gather_fusion.1, bf16[4,32,128,128]{2,3,1,0:T(8,128)(2,1)} %get-tuple-element.257, s32[]{:T(128)} %get-tuple-element.246), kind=kOutput, calls=%fused_computation.19.clone.1 | convolution fusion | flops 538968064 | bytes 13632128 | tf_op jit(solution)/shard_map/while/body/eval_jaxpr/tpq,tpf->tqf/dot_general | solution.py:35
  486.6 18.6 %scatter_fusion.1 = f32[16,128,512]{2,1,0:T(8,128)} fusion(f32[16,128,512]{2,1,0:T(8,128)} %get-tuple-element.247, s32[32]{0:T(128)S(1)} %get-tuple-element.212, f32[32,128,512]{2,1,0:T(8,128)} %broadcast_multiply_fusion.6), kind=kCustom, calls=%fused_computation.3.clone.1 | custom fusion | flops 2097152 | bytes 25165952 | tf_op jit(solution)/shard_map/while/body/eval_jaxpr/scatter-add | solution.py:39
  505.2 2.0 multiply_convert_fusion.1
  507.2 22.2 %all-reduce.3.cloned.1.call-done = f32[512,512]{1,0:T(8,128)} async-done(((f32[512,512]{1,0:T(8,128)}), f32[512,512]{1,0:T(8,128)}) %all-reduce.3.cloned.1.call-update) | async-done | bytes 1048592 | tf_op jit(solution)/shard_map/psum | solution.py:77
  529.3 2.3 broadcast_multiply_fusion.2
  531.6 83.7 %reduce-scatter.2.cloned.1.call-done = f32[256,512]{1,0:T(8,128)} async-done(((f32[2048,512]{1,0:T(8,128)}), f32[256,512]{1,0:T(8,128)}) %reduce-scatter.2.cloned.1.call-update) | async-done | bytes 524304 | tf_op jit(solution)/shard_map/reduce_scatter | solution.py:80
  615.3 1.8 convert_element_type.43
  (36 shorter events, 0.3 us)
Async XLA Ops:
  7.2 358.4 %copy-start = (bf16[512,512]{1,0:T(8,128)(2,1)S(1)}, bf16[512,512]{1,0:T(8,128)(2,1)}, u32[]{:S(2)}) copy-start(bf16[512,512]{1,0:T(8,128)(2,1)} %param.12) | copy-start | bytes 1572868
  7.2 57.6 %all-gather.3.cloned.1.call-start = ((), (), s32[]{:S(2)}) async-start(), calls=%async_computation.1 | async-start | bytes 2359296 | tf_op jit(solution)/shard_map/all_gather | solution.py:61
  7.9 357.6 %all-gather.5.cloned.1.call-start = ((), (), s32[]{:S(2)}) async-start(), calls=%async_computation.2 | async-start | bytes 4456448 | tf_op jit(solution)/shard_map/all_gather | solution.py:65
  8.7 520.7 %all-reduce.3.cloned.1.call-start = ((), (), s32[]{:S(2)}) async-start(), calls=%async_computation.3 | async-start | bytes 2097152 | tf_op jit(solution)/shard_map/psum | solution.py:77
  64.8 4.3 copy-start.2
  380.7 234.6 %reduce-scatter.2.cloned.1.call-start = ((), (), s32[]{:S(2)}) async-start(), calls=%async_computation.4 | async-start | bytes 4718592 | tf_op jit(solution)/shard_map/reduce_scatter | solution.py:80
  505.2 111.9 %copy-start.1 = (bf16[512,512]{1,0:T(8,128)(2,1)S(1)}, bf16[512,512]{1,0:T(8,128)(2,1)}, u32[]{:S(2)}) copy-start(bf16[512,512]{1,0:T(8,128)(2,1)} %param.12) | copy-start | bytes 1572868
Sparse Core Ops, SparseCore 0:
  10.4 54.4 all-gather.2
  66.5 39.2 all-gather.4
  380.9 148.4 all-reduce.2
  533.5 81.7 reduce-scatter.1
where the time goes:
time: 628 us; the launch traced here: 624 us
  blocking collectives  182 us (29%)
  other arithmetic  158 us (25%)
  waiting for transfers between devices  153 us (24%)
  matrix products  70.9 us (11%)
  local copies, waits for them, and re-layouts  44.9 us (7%)
  between operations  14.4 us (2%)
    psum x1, blocking collectives, local(): summed = lax.psum(partial_value, 'row')  182 us
    scatter-add x8, other arithmetic, one_group(): return (running.at[group_place].add(weighted), None)  149 us
    reduce_scatter x1, waiting for transfers between devices, local(): lax.psum_scatter(back_partial, 'col', scatter_dimension=0, tiled=True)  83.7 us
    all_gather x1, waiting for transfers between devices, local(): lax.all_gather(features, 'col', axis=0, tiled=True)  45.7 us
    gather x8, local copies, waits for them, and re-layouts, one_group(): picked = source[group_pick]  31 us
    dot_general x4, matrix products, one_group(): jnp.einsum('tpq,tqf->tpf', group_tiles, picked, preferred_element_type=jn...  27.9 us
    dot_general x4, matrix products, one_group(): jnp.einsum('tpq,tpf->tqf', group_tiles, picked, preferred_element_type=jn...  27.9 us
    psum x1, waiting for transfers between devices, local(): lax.psum(local_wgrad, ('row', 'col')) * float(node_total) ** (-0.5)  22.2 us
  transfers between devices with their start and end apart: 4, of which 3 were waited for; matrix products, arithmetic and copies ran while one was open for 41% of the time, Pallas kernels for 0%

commit v1 on v0

v1 whole, which is shorter than its diff:
```python
import jax
import jax.numpy as jnp
from jax import lax
from jax.experimental import pallas as pl
from jax.experimental.pallas import tpu as pltpu
from jax.sharding import Mesh, PartitionSpec as P

BF = jnp.bfloat16
F32 = jnp.float32
CHUNK = 32
UNROLL = 16


def tile_sums(forward, counts, rows, cols, own, sib, source, out_blocks):
    slots, side, _ = own.shape
    width = source.shape[-1]
    turns = slots // CHUNK

    def kernel(counts, rows, cols, own, sib, source, out, total):
        step = pl.program_id(0)

        @pl.when(step == 0)
        def _():
            total[...] = jnp.zeros_like(total)

        def chunk_sums(which, held, chunk):
            live = jnp.clip(counts[which] - chunk * CHUNK, 0, CHUNK)

            def one(place, carry):
                slot = chunk * CHUNK + place
                r, c = rows[which, slot], cols[which, slot]
                if forward:
                    total[r] += jnp.dot(held[place], source[c], preferred_element_type=F32)
                else:
                    total[c] += lax.dot_general(
                        held[place], source[r], (((0,), (0,)), ((), ())), preferred_element_type=F32
                    )
                return carry

            def several(group, carry):
                for u in range(UNROLL):
                    one(group * UNROLL + u, 0)
                return carry

            full = live // UNROLL
            lax.fori_loop(0, full, several, 0)
            lax.fori_loop(full * UNROLL, live, one, 0)

        @pl.when(step < turns)
        def _():
            chunk_sums(0, own, step)

        @pl.when(step >= turns)
        def _():
            chunk_sums(1, sib, step - turns)

        @pl.when(step == 2 * turns - 1)
        def _():
            out[...] = total[...].astype(BF)

    def own_at(i, counts, *_):
        return (jnp.minimum(jnp.minimum(i, turns - 1), jnp.maximum(counts[0] - 1, 0) // CHUNK), 0, 0)

    def sib_at(i, counts, *_):
        return (jnp.minimum(jnp.maximum(i - turns, 0), jnp.maximum(counts[1] - 1, 0) // CHUNK), 0, 0)

    shape = (out_blocks, side, width)
    return pl.pallas_call(
        kernel,
        grid_spec=pltpu.PrefetchScalarGridSpec(
            num_scalar_prefetch=3,
            grid=(2 * turns,),
            in_specs=[
                pl.BlockSpec((CHUNK, side, side), own_at),
                pl.BlockSpec((CHUNK, side, side), sib_at),
                pl.BlockSpec(source.shape, lambda i, *_: (0, 0, 0)),
            ],
            out_specs=pl.BlockSpec(shape, lambda i, *_: (0, 0, 0)),
            scratch_shapes=[pltpu.VMEM(shape, F32)],
        ),
        out_shape=jax.ShapeDtypeStruct(shape, BF),
        compiler_params=pltpu.CompilerParams(
            vmem_limit_bytes=40 << 20, dimension_semantics=("arbitrary",)
        ),
        cost_estimate=pl.CostEstimate(
            flops=4 * slots * side * side * width, bytes_accessed=16 << 20, transcendentals=0
        ),
        name="forward_tiles" if forward else "backward_tiles",
    )(counts, rows, cols, own, sib, source)


def middle(parts, weight, cotangent):
    chips, cores, own_rows, half = parts.shape
    width = cores * half

    def kernel(parts, weight, cot, act, grad, wgrad):
        w = weight[...]
        mixed = jnp.concatenate(
            [jnp.sum(parts[:, s].astype(F32), axis=0).astype(BF) for s in range(cores)], axis=1
        )
        pre = jnp.dot(mixed, w, preferred_element_type=F32)
        sig = jax.nn.sigmoid(pre)
        act[...] = (pre * sig).astype(BF)
        slope = sig * (1.0 + pre * (1.0 - sig))
        grad_pre = (cot[...].astype(F32) * slope).astype(BF)
        wgrad[...] = lax.dot_general(
            mixed, grad_pre, (((0,), (0,)), ((), ())), preferred_element_type=F32
        )
        mixed_grad = lax.dot_general(
            grad_pre, w, (((1,), (1,)), ((), ())), preferred_element_type=F32
        ).astype(BF)
        for s in range(cores):
            piece = mixed_grad[:, s * half : (s + 1) * half]
            for chip in range(chips):
                grad[chip, s] = piece

    return pl.pallas_call(
        kernel,
        out_shape=(
            jax.ShapeDtypeStruct((own_rows, width), BF),
            jax.ShapeDtypeStruct(parts.shape, BF),
            jax.ShapeDtypeStruct((width, width), F32),
        ),
        compiler_params=pltpu.CompilerParams(vmem_limit_bytes=40 << 20),
        cost_estimate=pl.CostEstimate(
            flops=6 * own_rows * width * width, bytes_accessed=7 << 20, transcendentals=own_rows * width
        ),
        name="middle",
    )(parts, weight, cotangent)


def local(features, weight, cotangent, tiles, tile_rows, tile_cols, tile_count):
    slots, side = tiles.shape[2], tiles.shape[3]
    own_rows, width = features.shape
    cores = lax.axis_size("core")
    chips = lax.axis_size("chip")
    cols = lax.axis_size("col")
    half = width // cores
    own_blocks = own_rows // side
    col_blocks = own_blocks * cols
    row_blocks = own_blocks * cores * chips
    nodes = own_rows * cores * chips * cols
    core = lax.axis_index("core")

    swap = [(0, 1), (1, 0)]
    own = tiles[0, 0]
    sib = lax.ppermute(own, "core", swap)
    ids = jnp.stack(
        [
            tile_rows[0, 0],
            tile_cols[0, 0] + core * col_blocks,
            jnp.broadcast_to(tile_count[0, 0], (slots,)),
        ]
    )
    both = jnp.stack([ids, lax.ppermute(ids, "core", swap)])
    row_ids, col_ids, counts = both[:, 0], both[:, 1], both[:, 2, 0]

    halves = features.reshape(own_rows, cores, half).transpose(1, 0, 2)
    sent = jnp.broadcast_to(halves[:, None], (cores, cols, own_rows, half))
    sent = sent.reshape(cores * cols, own_rows, half)
    stripe = lax.all_to_all(sent, ("core", "col"), 0, 0, tiled=True)
    stripe = stripe.reshape(cores * col_blocks, side, half)
    partial_sums = tile_sums(True, counts, row_ids, col_ids, own, sib, stripe, row_blocks)
    partial_sums = partial_sums.reshape(chips * cores, own_rows, half)
    parts = lax.all_to_all(partial_sums, ("chip", "core"), 0, 0, tiled=True)
    act, grad, wgrad = middle(parts.reshape(chips, cores, own_rows, half), weight, cotangent)

    wgrad = lax.psum_scatter(wgrad, ("chip", "core"), scatter_dimension=0, tiled=True)
    wgrad = lax.psum(wgrad, "col") * float(nodes) ** (-0.5)
    wgrad = lax.all_gather(wgrad, ("chip", "core"), axis=0, tiled=True)

    grad = lax.all_to_all(
        grad.reshape(chips * cores, own_rows, half), ("chip", "core"), 0, 0, tiled=True
    )
    grad = grad.reshape(row_blocks, side, half)
    back = tile_sums(False, counts, row_ids, col_ids, own, sib, grad, cores * col_blocks)
    back = lax.all_to_all(
        back.reshape(cores * cols, own_rows, half), ("core", "col"), 0, 0, tiled=True
    )
    back = back.reshape(cores, cols, own_rows, half).astype(F32).sum(1).astype(BF)
    return act, wgrad, back.transpose(1, 0, 2).reshape(own_rows, width)


def solution(mesh):
    rows, cols = mesh.devices.shape
    fine = Mesh(mesh.devices.reshape(rows // 2, 2, cols), ("chip", "core", "col"))
    row = ("chip", "core")
    in_specs = (
        P((*row, "col"), None),
        P(),
        P(("col", *row), None),
        P(row, "col", None, None, None),
        P(row, "col", None),
        P(row, "col", None),
        P(row, "col", None),
    )
    out_specs = (P(("col", *row), None), P(), P((*row, "col"), None))
    return jax.shard_map(local, mesh=fine, in_specs=in_specs, out_specs=out_specs, check_vma=False)
```

time: 628 us -> 307 us (0.49)
  other arithmetic: 158 us -> 1.95 us
  blocking collectives: 182 us -> 33.1 us
  matrix products: 70.9 us -> 0 us
  waiting for transfers between devices: 153 us -> 199 us
  local copies, waits for them, and re-layouts: 44.9 us -> 13 us
  starting transfers between devices: 0.34 us -> 26 us
  Pallas kernels: 0 us -> 16.7 us
    psum x1 -> x0, blocking collectives: 182 us -> none  [local(): summed = lax.psum(partial_value, 'row')]
    scatter-add x8 -> x0, other arithmetic: 149 us -> none  [one_group(): return (running.at[group_place].add(weighted), None)]
    dot_general x11 -> x0, matrix products: 70.9 us -> none  [the longest x4 27.9 us: one_group(): jnp.einsum('tpq,tqf->tpf', group_tiles, picked, preferred_element_type=jn...]
    psum x1, waiting for transfers between devices: 22.2 us -> 69.7 us  [local(): wgrad = lax.psum(wgrad, 'col') * float(nodes) ** (-0.5)]
    all_to_all x0 -> x1, blocking collectives: none -> 33.1 us  [local(): parts = lax.all_to_all(partial_sums, ('chip', 'core'), 0, 0, tiled=True)]
    gather x8 -> x0, local copies, waits for them, and re-layouts: 31 us -> none  [one_group(): picked = source[group_pick]]
    all_to_all x0 -> x3, waiting for transfers between devices: none -> 26.9 us  [the longest x1 26.9 us: local(): stripe = lax.all_to_all(sent, ('core', 'col'), 0, 0, tiled=True)]
    all_to_all x0 -> x3, starting transfers between devices: none -> 24.7 us  [the longest x1 11.9 us: local(): lax.all_to_all(back.reshape(cores * cols, own_rows, half), ('core', 'col'...]
  transfers between devices with their start and end apart: 4 -> 8, of which waited for: 3 -> 5; matrix products, arithmetic and copies ran while one was open for 41% -> 2% of each run, Pallas kernels for 0% -> 2%
where the time goes in v1:
time: 307 us; the launch traced here: 304 us
  waiting for transfers between devices  199 us (65%)
  blocking collectives  33.1 us (11%)
  starting transfers between devices  26 us (8%)
  Pallas kernels  16.7 us (5%)
  between operations  14.5 us (5%)
  local copies, waits for them, and re-layouts  13 us (4%)
    psum x1, waiting for transfers between devices, local(): wgrad = lax.psum(wgrad, 'col') * float(nodes) ** (-0.5)  69.7 us
    reduce_scatter x1, waiting for transfers between devices, local(): lax.psum_scatter(wgrad, ('chip', 'core'), scatter_dimension=0, tiled=True)  64.1 us
    all_gather x1, waiting for transfers between devices, local(): wgrad = lax.all_gather(wgrad, ('chip', 'core'), axis=0, tiled=True)  37.4 us
    all_to_all x1, blocking collectives, local(): parts = lax.all_to_all(partial_sums, ('chip', 'core'), 0, 0, tiled=True)  33.1 us
    all_to_all x1, waiting for transfers between devices, local(): stripe = lax.all_to_all(sent, ('core', 'col'), 0, 0, tiled=True)  26.9 us
    pallas_call x2, Pallas kernels, tile_sums(): pl.pallas_call(kernel, grid_spec=pltpu.PrefetchScalarGridSpec(num_scalar_...  14.9 us
    all_to_all x1, starting transfers between devices, local(): lax.all_to_all(back.reshape(cores * cols, own_rows, half), ('core', 'col'...  11.9 us
    unnamed x18, local copies, waits for them, and re-layouts  10.2 us
  transfers between devices with their start and end apart: 8, of which 5 were waited for; matrix products, arithmetic and copies ran while one was open for 2% of the time, Pallas kernels for 2%

profile of v1, /device:TPU:17, one launch (start us, length us, event | category | flops | bytes accessed | tf_op | source)
XLA Modules:
  0.0 304.2 jit_solution(18051642122164943909)
XLA Ops:
  7.2 0.8 collective-permute-start.1
  7.9 1.0 reshape.53
  9.0 1.6 broadcast_in_dim.2
  10.5 0.0 copy-start.7
  10.5 0.0 copy-start.6
  10.5 8.0 %all-to-all-start = ((bf16[16,256,256]{2,1,0:T(8,128)(2,1)}), bf16[16,256,256]{2,1,0:T(8,128)(2,1)S(1)}, u32[]{:S(2)}, u32[]{:S(2)}) async-start(bf16[16,256,256]{2,1,0:T(8,128)(2,1)} %bitcast.35), calls=%async_computation | async-start | bytes 4194304 | tf_op jit(solution)/shard_map/all_to_all | solution.py:161
  18.6 0.0 reduce-scatter.2.cloned.1.call-start
  19.3 0.1 pad.4.clone
  19.3 0.0 copy-done.7
  19.3 0.0 copy-done.6
  19.3 0.1 fusion.5
  19.4 0.4 collective-permute-start
  19.8 0.8 collective-permute-done
  20.6 0.1 fusion.4.counts
  20.7 26.9 %all-to-all-done = bf16[16,256,256]{2,1,0:T(8,128)(2,1)S(1)} async-done(((bf16[16,256,256]{2,1,0:T(8,128)(2,1)}), bf16[16,256,256]{2,1,0:T(8,128)(2,1)S(1)}, u32[]{:S(2)}, u32[]{:S(2)}) %all-to-all-start) | async-done | bytes 2097184 | tf_op jit(solution)/shard_map/all_to_all | solution.py:161
  47.6 0.0 collective-permute-done.1.sib
  47.6 0.0 copy-start
  47.6 2.2 copy-done
  49.8 7.4 %forward_tiles.1 = bf16[32,128,256]{2,1,0:T(8,128)(2,1)S(1)} custom-call(s32[2]{0:T(128)S(1)} %fusion.4.counts, s32[2,128]{1,0:T(2,128)S(1)} %get-tuple-element.13.rows, s32[2,128]{1,0:T(2,128)S(1)} %get-tuple-element.12.cols, bf16[128,128,128]{2,1,0:T(8,128)(2,1)S(1)} %bitcast.27, bf16[128,128,128]{2,1,0:T(8,128)(2,1)} %collective-permute-done.1.sib, ...), custom_call_target="tpu_custom_call" | custom-call | flops 2147483648 | bytes 16777216 | tf_op jit(solution)/shard_map/forward_tiles/pallas_call | solution.py:68
  57.2 0.0 copy-start.4
  57.2 0.0 copy-start.5
  57.2 33.1 %all_to_all.20 = bf16[16,256,256]{2,1,0:T(8,128)(2,1)S(1)} all-to-all(bf16[16,256,256]{2,1,0:T(8,128)(2,1)S(1)} %bitcast.33), channel_id=1, replica_groups=mesh['chip'=8,'core'=2,'col'=8] {'chip','core'}, dimensions={0} | all-to-all | bytes 4194304 | tf_op jit(solution)/shard_map/all_to_all | solution.py:165
  90.3 0.0 copy-done.4
  90.3 0.0 copy-done.5
  90.3 1.7 middle.1
  92.1 1.4 copy-done.3
  93.4 0.0 reduce-scatter.2.cloned.1.call-update
  93.5 4.8 %all-to-all-start.2 = ((bf16[16,256,256]{2,1,0:T(8,128)(2,1)}), bf16[16,256,256]{2,1,0:T(8,128)(2,1)S(1)}, u32[]{:S(2)}, u32[]{:S(2)}) async-start(bf16[16,256,256]{2,1,0:T(8,128)(2,1)} %bitcast.34), calls=%async_computation.3 | async-start | bytes 4194304 | tf_op jit(solution)/shard_map/all_to_all | solution.py:172
  98.3 0.0 all-reduce.2.cloned.1.call-start
  98.3 64.1 %reduce-scatter.2.cloned.1.call-done = f32[32,512]{1,0:T(8,128)} async-done(((f32[512,512]{1,0:T(8,128)}), f32[32,512]{1,0:T(8,128)}) %reduce-scatter.2.cloned.1.call-update) | async-done | bytes 65552 | tf_op jit(solution)/shard_map/reduce_scatter | solution.py:168
  162.5 0.0 all-reduce.2.cloned.1.call-update
  162.5 0.0 all-to-all-done.2
  162.5 0.0 copy-start.1
  162.5 2.2 copy-done.1
  164.7 7.6 %backward_tiles.1 = bf16[32,128,256]{2,1,0:T(8,128)(2,1)S(1)} custom-call(s32[2]{0:T(128)S(1)} %fusion.4.counts, s32[2,128]{1,0:T(2,128)S(1)} %get-tuple-element.13.rows, s32[2,128]{1,0:T(2,128)S(1)} %get-tuple-element.12.cols, bf16[128,128,128]{2,1,0:T(8,128)(2,1)S(1)} %bitcast.28, bf16[128,128,128]{2,1,0:T(8,128)(2,1)} %collective-permute-done.1.sib, ...), custom_call_target="tpu_custom_call" | custom-call | flops 2147483648 | bytes 16777216 | tf_op jit(solution)/shard_map/backward_tiles/pallas_call | solution.py:68
  172.3 0.0 copy-start.2
  172.3 1.3 copy-done.2
  173.6 11.9 %all-to-all-start.3 = ((bf16[16,256,256]{2,1,0:T(8,128)(2,1)}), bf16[16,256,256]{2,1,0:T(8,128)(2,1)S(1)}, u32[]{:S(2)}, u32[]{:S(2)}) async-start(bf16[16,256,256]{2,1,0:T(8,128)(2,1)} %bitcast.32), calls=%async_computation.4 | async-start | bytes 4194304 | tf_op jit(solution)/shard_map/all_to_all | solution.py:177
  185.5 0.0 all-gather.2.cloned.1.call-start
  185.5 69.7 %all-reduce.2.cloned.1.call-done = f32[32,512]{1,0:T(8,128)} async-done(((f32[32,512]{1,0:T(8,128)}), f32[32,512]{1,0:T(8,128)}) %all-reduce.2.cloned.1.call-update) | async-done | bytes 65552 | tf_op jit(solution)/shard_map/psum | solution.py:169
  255.2 1.5 broadcast_multiply_fusion
  256.7 0.0 all-gather.2.cloned.1.call-update
  256.7 0.0 all-to-all-done.3
  256.7 0.3 bitcast_reduce_fusion
  257.0 0.1 copy.18
  257.2 0.8 copy.19
  258.0 37.4 %all-gather.2.cloned.1.call-done = f32[512,512]{1,0:T(8,128)} async-done(((f32[32,512]{1,0:T(8,128)}), f32[512,512]{1,0:T(8,128)}) %all-gather.2.cloned.1.call-update) | async-done | bytes 1048592 | tf_op jit(solution)/shard_map/all_gather | solution.py:170
  295.4 2.3 copy.23
  (6 shorter events, 0.0 us)
Async XLA Ops:
  7.2 40.4 %collective-permute-start.1 = (bf16[128,128,128]{2,1,0:T(8,128)(2,1)}, bf16[128,128,128]{2,1,0:T(8,128)(2,1)}, u32[]{:S(2)}, u32[]{:S(2)}) collective-permute-start(bf16[128,128,128]{2,1,0:T(8,128)(2,1)} %bitcast.26), channel_id=1, source_target_pairs={{0,8},{8,0},{1,9},{9,1},{2,10},{10,2},{3,11},{11,3},{4,12},{12,4},... | collective-permute-start | bytes 12582920 | tf_op jit(solution)/shard_map/ppermute | solution.py:147
  10.5 8.8 %copy-start.7 = (s32[1,1,128]{2,1,0:T(1,128)S(1)}, s32[1,1,128]{2,1,0:T(1,128)}, u32[]{:S(2)}) copy-start(s32[1,1,128]{2,1,0:T(1,128)} %param.12) | copy-start | bytes 1540
  10.5 8.8 %copy-start.6 = (s32[1,1,128]{2,1,0:T(1,128)S(1)}, s32[1,1,128]{2,1,0:T(1,128)}, u32[]{:S(2)}) copy-start(s32[1,1,128]{2,1,0:T(1,128)} %param.11) | copy-start | bytes 1540
  10.5 37.1 %all-to-all-start = ((bf16[16,256,256]{2,1,0:T(8,128)(2,1)}), bf16[16,256,256]{2,1,0:T(8,128)(2,1)S(1)}, u32[]{:S(2)}, u32[]{:S(2)}) async-start(bf16[16,256,256]{2,1,0:T(8,128)(2,1)} %bitcast.35), calls=%async_computation | async-start | bytes 4194304 | tf_op jit(solution)/shard_map/all_to_all | solution.py:161
  18.6 143.9 %reduce-scatter.2.cloned.1.call-start = ((), (), s32[]{:S(2)}) async-start(), calls=%async_computation.5 | async-start | bytes 1114112 | tf_op jit(solution)/shard_map/reduce_scatter | solution.py:168
  19.4 1.2 collective-permute-start
  47.6 2.2 copy-start
  57.2 33.2 %copy-start.4 = (bf16[512,512]{1,0:T(8,128)(2,1)S(1)}, bf16[512,512]{1,0:T(8,128)(2,1)}, u32[]{:S(2)}) copy-start(bf16[512,512]{1,0:T(8,128)(2,1)} %weight.1) | copy-start | bytes 1572868
  57.2 33.2 %copy-start.5 = (bf16[256,512]{1,0:T(8,128)(2,1)S(1)}, bf16[256,512]{1,0:T(8,128)(2,1)}, u32[]{:S(2)}) copy-start(bf16[256,512]{1,0:T(8,128)(2,1)} %cot.1) | copy-start | bytes 786436
  92.1 1.4 copy-start.3
  93.5 69.1 %all-to-all-start.2 = ((bf16[16,256,256]{2,1,0:T(8,128)(2,1)}), bf16[16,256,256]{2,1,0:T(8,128)(2,1)S(1)}, u32[]{:S(2)}, u32[]{:S(2)}) async-start(bf16[16,256,256]{2,1,0:T(8,128)(2,1)} %bitcast.34), calls=%async_computation.3 | async-start | bytes 4194304 | tf_op jit(solution)/shard_map/all_to_all | solution.py:172
  98.3 156.9 %all-reduce.2.cloned.1.call-start = ((), (), s32[]{:S(2)}) async-start(), calls=%async_computation.6 | async-start | bytes 131072 | tf_op jit(solution)/shard_map/psum | solution.py:169
  162.5 2.2 copy-start.1
  172.3 1.3 copy-start.2
  173.6 83.1 %all-to-all-start.3 = ((bf16[16,256,256]{2,1,0:T(8,128)(2,1)}), bf16[16,256,256]{2,1,0:T(8,128)(2,1)S(1)}, u32[]{:S(2)}, u32[]{:S(2)}) async-start(bf16[16,256,256]{2,1,0:T(8,128)(2,1)} %bitcast.32), calls=%async_computation.4 | async-start | bytes 4194304 | tf_op jit(solution)/shard_map/all_to_all | solution.py:177
  185.5 109.9 %all-gather.2.cloned.1.call-start = ((), (), s32[]{:S(2)}) async-start(), calls=%async_computation.7 | async-start | bytes 1114112 | tf_op jit(solution)/shard_map/all_gather | solution.py:170
Sparse Core Ops, SparseCore 0:
  93.6 68.8 reduce-scatter.1
  165.1 90.0 all-reduce.1
  257.5 37.8 all-gather.1

commit v2 on v1

--- a/solution.py
+++ b/solution.py
@@ -7,8 +7,8 @@
 
 BF = jnp.bfloat16
 F32 = jnp.float32
-CHUNK = 32
-UNROLL = 16
+CHUNK = 64
+UNROLL = 32
 
 
 def tile_sums(forward, counts, rows, cols, own, sib, source, out_blocks):
@@ -92,8 +92,9 @@
 def middle(parts, weight, cotangent):
     chips, cores, own_rows, half = parts.shape
     width = cores * half
-
-    def kernel(parts, weight, cot, act, grad, wgrad):
+    share = width // (chips * cores)
+
+    def kernel(parts, weight, cot, act, grad):
         w = weight[...]
         mixed = jnp.concatenate(
             [jnp.sum(parts[:, s].astype(F32), axis=0).astype(BF) for s in range(cores)], axis=1
@@ -103,23 +104,27 @@
         act[...] = (pre * sig).astype(BF)
         slope = sig * (1.0 + pre * (1.0 - sig))
         grad_pre = (cot[...].astype(F32) * slope).astype(BF)
-        wgrad[...] = lax.dot_general(
+        wgrad = lax.dot_general(
             mixed, grad_pre, (((0,), (0,)), ((), ())), preferred_element_type=F32
-        )
+        ).astype(BF)
         mixed_grad = lax.dot_general(
             grad_pre, w, (((1,), (1,)), ((), ())), preferred_element_type=F32
         ).astype(BF)
         for s in range(cores):
             piece = mixed_grad[:, s * half : (s + 1) * half]
             for chip in range(chips):
-                grad[chip, s] = piece
+                grad[chip, s, :own_rows] = piece
+                at = (chip * cores + s) * share
+                for h in range(cores):
+                    grad[chip, s, own_rows + h * share : own_rows + (h + 1) * share] = wgrad[
+                        at : at + share, h * half : (h + 1) * half
+                    ]
 
     return pl.pallas_call(
         kernel,
         out_shape=(
             jax.ShapeDtypeStruct((own_rows, width), BF),
-            jax.ShapeDtypeStruct(parts.shape, BF),
-            jax.ShapeDtypeStruct((width, width), F32),
+            jax.ShapeDtypeStruct((chips, cores, own_rows + cores * share, half), BF),
         ),
         compiler_params=pltpu.CompilerParams(vmem_limit_bytes=40 << 20),
         cost_estimate=pl.CostEstimate(
@@ -163,16 +168,27 @@
     partial_sums = tile_sums(True, counts, row_ids, col_ids, own, sib, stripe, row_blocks)
     partial_sums = partial_sums.reshape(chips * cores, own_rows, half)
     parts = lax.all_to_all(partial_sums, ("chip", "core"), 0, 0, tiled=True)
-    act, grad, wgrad = middle(parts.reshape(chips, cores, own_rows, half), weight, cotangent)
-
-    wgrad = lax.psum_scatter(wgrad, ("chip", "core"), scatter_dimension=0, tiled=True)
-    wgrad = lax.psum(wgrad, "col") * float(nodes) ** (-0.5)
-    wgrad = lax.all_gather(wgrad, ("chip", "core"), axis=0, tiled=True)
-
-    grad = lax.all_to_all(
-        grad.reshape(chips * cores, own_rows, half), ("chip", "core"), 0, 0, tiled=True
-    )
-    grad = grad.reshape(row_blocks, side, half)
+    act, grad = middle(parts.reshape(chips, cores, own_rows, half), weight, cotangent)
+
+    exchanged = lax.all_to_all(
+        grad.reshape(chips * cores, -1, half), ("chip", "core"), 0, 0, tiled=True
+    )
+    grad = exchanged[:, :own_rows].reshape(row_blocks, side, half)
+    wgrad = exchanged[:, own_rows:].astype(F32).sum(0) * float(nodes) ** (-0.5)
+    wgrad = jnp.broadcast_to(wgrad[None], (cols, *wgrad.shape))
+    wgrad = lax.all_to_all(wgrad, "col", 0, 0, tiled=True).sum(0)
+    wgrad = jnp.concatenate([wgrad[: wgrad.shape[0] // 2], wgrad[wgrad.shape[0] // 2 :]], axis=1)
+    other = lax.ppermute(wgrad, "core", swap)
+    wgrad = jnp.where(core == 0, jnp.concatenate([wgrad, other]), jnp.concatenate([other, wgrad]))
+    chip = lax.axis_index("chip")
+    gathered = jnp.zeros((chips, *wgrad.shape), F32)
+    for away in range(chips):
+        piece = wgrad
+        if away:
+            piece = lax.ppermute(wgrad, "chip", [(i, i ^ away) for i in range(chips)])
+        gathered = lax.dynamic_update_slice(gathered, piece[None], (chip ^ away, 0, 0))
+    wgrad = gathered.reshape(width, width)
+
     back = tile_sums(False, counts, row_ids, col_ids, own, sib, grad, cores * col_blocks)
     back = lax.all_to_all(
         back.reshape(cores * cols, own_rows, half), ("core", "col"), 0, 0, tiled=True

time: 307 us -> 195 us (0.64)
  waiting for transfers between devices: 199 us -> 57 us
  blocking collectives: 33.1 us -> 69.7 us
  between operations: 14.5 us -> 1.56 us
  starting transfers between devices: 26 us -> 36.3 us
    psum x1 -> x0, waiting for transfers between devices: 69.7 us -> none  [local(): wgrad = lax.psum(wgrad, 'col') * float(nodes) ** (-0.5)]
    reduce_scatter x1 -> x0, waiting for transfers between devices: 64.1 us -> none  [local(): lax.psum_scatter(wgrad, ('chip', 'core'), scatter_dimension=0, tiled=True)]
    all_gather x1 -> x0, waiting for transfers between devices: 37.4 us -> none  [local(): wgrad = lax.all_gather(wgrad, ('chip', 'core'), axis=0, tiled=True)]
    all_to_all x0 -> x1, blocking collectives: none -> 35.9 us  [local(): lax.all_to_all(grad.reshape(chips * cores, -1, half), ('chip', 'core'), 0...]
    ppermute x0 -> x8, waiting for transfers between devices: none -> 29.2 us  [the longest x7 28.3 us: local(): piece = lax.ppermute(wgrad, 'chip', [(i, i ^ away) for i in range(chips)])]
    ppermute x0 -> x8, starting transfers between devices: none -> 10.7 us  [the longest x7 10.3 us: local(): piece = lax.ppermute(wgrad, 'chip', [(i, i ^ away) for i in range(chips)])]
    unnamed x18 -> x17, local copies, waits for them, and re-layouts: 10.2 us -> 5.46 us
  transfers between devices with their start and end apart: 8 -> 13, of which waited for: 5 -> 5; matrix products, arithmetic and copies ran while one was open for 2% -> 3% of each run, Pallas kernels for 2% -> 4%
where the time goes in v2:
time: 195 us; the launch traced here: 193 us
  blocking collectives  69.7 us (36%)
  waiting for transfers between devices  57 us (29%)
  starting transfers between devices  36.3 us (19%)
  Pallas kernels  15.7 us (8%)
  local copies, waits for them, and re-layouts  12.2 us (6%)
    all_to_all x1, blocking collectives, local(): lax.all_to_all(grad.reshape(chips * cores, -1, half), ('chip', 'core'), 0...  35.9 us
    all_to_all x1, blocking collectives, local(): parts = lax.all_to_all(partial_sums, ('chip', 'core'), 0, 0, tiled=True)  33.8 us
    ppermute x7, waiting for transfers between devices, local(): piece = lax.ppermute(wgrad, 'chip', [(i, i ^ away) for i in range(chips)])  28.3 us
    all_to_all x1, waiting for transfers between devices, local(): stripe = lax.all_to_all(sent, ('core', 'col'), 0, 0, tiled=True)  26.9 us
    pallas_call x2, Pallas kernels, tile_sums(): pl.pallas_call(kernel, grid_spec=pltpu.PrefetchScalarGridSpec(num_scalar_...  14.3 us
    all_to_all x1, starting transfers between devices, local(): lax.all_to_all(back.reshape(cores * cols, own_rows, half), ('core', 'col'...  10.5 us
    ppermute x7, starting transfers between devices, local(): piece = lax.ppermute(wgrad, 'chip', [(i, i ^ away) for i in range(chips)])  10.3 us
    all_to_all x1, starting transfers between devices, local(): stripe = lax.all_to_all(sent, ('core', 'col'), 0, 0, tiled=True)  8.02 us
  transfers between devices with their start and end apart: 13, of which 5 were waited for; matrix products, arithmetic and copies ran while one was open for 3% of the time, Pallas kernels for 4%

profile of v2, /device:TPU:17, one launch (start us, length us, event | category | flops | bytes accessed | tf_op | source)
XLA Modules:
  0.0 193.0 jit_solution(17623015692855258459)
XLA Ops:
  0.6 0.8 collective-permute-start.1
  1.4 1.0 reshape.114
  2.4 1.6 broadcast_in_dim.37
  4.0 8.0 %all-to-all-start = ((bf16[16,256,256]{2,1,0:T(8,128)(2,1)}), bf16[16,256,256]{2,1,0:T(8,128)(2,1)S(1)}, u32[]{:S(2)}, u32[]{:S(2)}) async-start(bf16[16,256,256]{2,1,0:T(8,128)(2,1)} %bitcast.52), calls=%async_computation | async-start | bytes 4194304 | tf_op jit(solution)/shard_map/all_to_all | solution.py:166
  12.7 0.1 pad.16.clone
  12.8 0.1 fusion.6
  12.8 0.4 collective-permute-start
  13.2 0.8 collective-permute-done
  14.0 0.1 fusion.5.counts
  14.2 26.9 %all-to-all-done = bf16[16,256,256]{2,1,0:T(8,128)(2,1)S(1)} async-done(((bf16[16,256,256]{2,1,0:T(8,128)(2,1)}), bf16[16,256,256]{2,1,0:T(8,128)(2,1)S(1)}, u32[]{:S(2)}, u32[]{:S(2)}) %all-to-all-start) | async-done | bytes 2097184 | tf_op jit(solution)/shard_map/all_to_all | solution.py:166
  41.1 0.0 collective-permute-done.1.sib
  41.1 2.2 %copy-done = bf16[1,1,128,128,128]{4,3,2,1,0:T(8,128)(2,1)S(1)} copy-done((bf16[1,1,128,128,128]{4,3,2,1,0:T(8,128)(2,1)S(1)}, bf16[1,1,128,128,128]{4,3,2,1,0:T(8,128)(2,1)}, u32[]{:S(2)}) %copy-start) | copy-done | bytes 4194328
  43.2 6.1 %forward_tiles.1 = bf16[32,128,256]{2,1,0:T(8,128)(2,1)S(1)} custom-call(s32[2]{0:T(128)S(1)} %fusion.5.counts, s32[2,128]{1,0:T(2,128)S(1)} %get-tuple-element.18.rows, s32[2,128]{1,0:T(2,128)S(1)} %get-tuple-element.17.cols, bf16[128,128,128]{2,1,0:T(8,128)(2,1)S(1)} %bitcast.45, bf16[128,128,128]{2,1,0:T(8,128)(2,1)} %collective-permute-done.1.sib, ...), custom_call_target="tpu_custom_call" | custom-call | flops 2147483648 | bytes 16777216 | tf_op jit(solution)/shard_map/forward_tiles/pallas_call | solution.py:68
  49.3 0.0 copy-start.2
  49.4 0.0 copy-start.3
  49.4 33.8 %all_to_all.25 = bf16[16,256,256]{2,1,0:T(8,128)(2,1)S(1)} all-to-all(bf16[16,256,256]{2,1,0:T(8,128)(2,1)S(1)} %bitcast.50), channel_id=1, replica_groups=mesh['chip'=8,'core'=2,'col'=8] {'chip','core'}, dimensions={0} | all-to-all | bytes 4194304 | tf_op jit(solution)/shard_map/all_to_all | solution.py:170
  83.1 1.4 middle.1
  84.5 35.9 %all_to_all.26 = bf16[16,320,256]{2,1,0:T(8,128)(2,1)S(1)} all-to-all(bf16[16,320,256]{2,1,0:T(8,128)(2,1)S(1)} %bitcast.51), channel_id=1, replica_groups=mesh['chip'=8,'core'=2,'col'=8] {'chip','core'}, dimensions={0} | all-to-all | bytes 5242880 | tf_op jit(solution)/shard_map/all_to_all | solution.py:173
  120.5 1.5 copy-done.4
  122.0 0.1 convert_reduce_fusion
  122.1 0.8 broadcast_in_dim.39
  122.9 5.9 %all-to-all-start.3 = ((f32[8,64,256]{2,1,0:T(8,128)}), f32[8,64,256]{2,1,0:T(8,128)S(1)}, u32[]{:S(2)}, u32[]{:S(2)}) async-start(f32[8,64,256]{2,1,0:T(8,128)} %broadcast_in_dim.39), calls=%async_computation.3 | async-start | bytes 1048576 | tf_op jit(solution)/shard_map/all_to_all | solution.py:179
  128.8 1.9 slice.35
  130.7 0.9 copy-done.1
  131.6 8.2 %backward_tiles.1 = bf16[32,128,256]{2,1,0:T(8,128)(2,1)} custom-call(s32[2]{0:T(128)S(1)} %fusion.5.counts, s32[2,128]{1,0:T(2,128)S(1)} %get-tuple-element.18.rows, s32[2,128]{1,0:T(2,128)S(1)} %get-tuple-element.17.cols, bf16[128,128,128]{2,1,0:T(8,128)(2,1)S(1)} %bitcast.46, bf16[128,128,128]{2,1,0:T(8,128)(2,1)} %collective-permute-done.1.sib, ...), custom_call_target="tpu_custom_call" | custom-call | flops 2147483648 | bytes 16777216 | tf_op jit(solution)/shard_map/backward_tiles/pallas_call | solution.py:68
  139.8 0.0 all-to-all-done.3
  139.8 10.5 %all-to-all-start.4 = ((bf16[16,256,256]{2,1,0:T(8,128)(2,1)}), bf16[16,256,256]{2,1,0:T(8,128)(2,1)S(1)}, u32[]{:S(2)}, u32[]{:S(2)}) async-start(bf16[16,256,256]{2,1,0:T(8,128)(2,1)} %bitcast.24), calls=%async_computation.4 | async-start | bytes 4194304 | tf_op jit(solution)/shard_map/all_to_all | solution.py:193
  150.4 0.4 collective-permute-start.2
  150.9 0.9 collective-permute-done.2
  151.8 0.1 collective-permute-start.3
  151.9 0.1 collective-permute-start.4
  152.0 2.5 %collective-permute-start.5 = (f32[64,512]{1,0:T(8,128)S(1)}, f32[64,512]{1,0:T(8,128)S(1)}, u32[]{:S(2)}, u32[]{:S(2)}) collective-permute-start(f32[64,512]{1,0:T(8,128)S(1)} %maximum_select_fusion.1), channel_id=1, source_target_pairs={{0,48},{16,32},{32,16},{48,0},{64,112},{80,96},{96,80},{112,64},{1... | collective-permute-start | bytes 393224 | tf_op jit(solution)/shard_map/ppermute | solution.py:188
  154.5 0.8 collective-permute-start.6
  155.3 2.0 %collective-permute-start.7 = (f32[64,512]{1,0:T(8,128)S(1)}, f32[64,512]{1,0:T(8,128)S(1)}, u32[]{:S(2)}, u32[]{:S(2)}) collective-permute-start(f32[64,512]{1,0:T(8,128)S(1)} %maximum_select_fusion.1), channel_id=1, source_target_pairs={{0,80},{16,64},{32,112},{48,96},{64,16},{80,0},{96,48},{112,32},{1... | collective-permute-start | bytes 393224 | tf_op jit(solution)/shard_map/ppermute | solution.py:188
  157.3 0.1 broadcast_in_dim.38
  157.5 24.0 %collective-permute-done.3 = f32[64,512]{1,0:T(8,128)} collective-permute-done((f32[64,512]{1,0:T(8,128)S(1)}, f32[64,512]{1,0:T(8,128)}, u32[]{:S(2)}, u32[]{:S(2)}) %collective-permute-start.3) | collective-permute-done | bytes 131104 | tf_op jit(solution)/shard_map/ppermute | solution.py:188
  181.5 1.1 collective-permute-start.8
  182.6 0.9 bitcast_dynamic-update-slice_fusion.6
  183.5 0.0 collective-permute-done.4
  183.5 3.7 %collective-permute-start.9 = (f32[64,512]{1,0:T(8,128)S(1)}, f32[64,512]{1,0:T(8,128)S(1)}, u32[]{:S(2)}, u32[]{:S(2)}) collective-permute-start(f32[64,512]{1,0:T(8,128)S(1)} %maximum_select_fusion.1), channel_id=1, source_target_pairs={{0,112},{16,96},{32,80},{48,64},{64,48},{80,32},{96,16},{112,0},{1... | collective-permute-start | bytes 393224 | tf_op jit(solution)/shard_map/ppermute | solution.py:188
  187.2 0.0 collective-permute-done.5
  187.2 0.0 collective-permute-done.6
  187.3 0.0 collective-permute-done.8
  187.3 4.3 %collective-permute-done.9 = f32[64,512]{1,0:T(8,128)S(1)} collective-permute-done((f32[64,512]{1,0:T(8,128)S(1)}, f32[64,512]{1,0:T(8,128)S(1)}, u32[]{:S(2)}, u32[]{:S(2)}) %collective-permute-start.9) | collective-permute-done | bytes 131104 | tf_op jit(solution)/shard_map/ppermute | solution.py:188
  191.7 0.0 copy-start.5
  191.7 0.3 bitcast_reduce_fusion
  192.0 0.1 copy.22
  192.1 0.8 copy.23
  (29 shorter events, 0.2 us)
Async XLA Ops:
  0.6 40.4 %collective-permute-start.1 = (bf16[128,128,128]{2,1,0:T(8,128)(2,1)}, bf16[128,128,128]{2,1,0:T(8,128)(2,1)}, u32[]{:S(2)}, u32[]{:S(2)}) collective-permute-start(bf16[128,128,128]{2,1,0:T(8,128)(2,1)} %bitcast.44), channel_id=1, source_target_pairs={{0,8},{8,0},{1,9},{9,1},{2,10},{10,2},{3,11},{11,3},{4,12},{12,4},... | collective-permute-start | bytes 12582920 | tf_op jit(solution)/shard_map/ppermute | solution.py:152
  4.0 8.8 %copy-start.7 = (s32[1,1,128]{2,1,0:T(1,128)S(1)}, s32[1,1,128]{2,1,0:T(1,128)}, u32[]{:S(2)}) copy-start(s32[1,1,128]{2,1,0:T(1,128)} %param.12) | copy-start | bytes 1540
  4.0 8.8 %copy-start.6 = (s32[1,1,128]{2,1,0:T(1,128)S(1)}, s32[1,1,128]{2,1,0:T(1,128)}, u32[]{:S(2)}) copy-start(s32[1,1,128]{2,1,0:T(1,128)} %param.11) | copy-start | bytes 1540
  4.0 37.1 %all-to-all-start = ((bf16[16,256,256]{2,1,0:T(8,128)(2,1)}), bf16[16,256,256]{2,1,0:T(8,128)(2,1)S(1)}, u32[]{:S(2)}, u32[]{:S(2)}) async-start(bf16[16,256,256]{2,1,0:T(8,128)(2,1)} %bitcast.52), calls=%async_computation | async-start | bytes 4194304 | tf_op jit(solution)/shard_map/all_to_all | solution.py:166
  12.8 1.2 collective-permute-start
  41.1 2.2 %copy-start = (bf16[1,1,128,128,128]{4,3,2,1,0:T(8,128)(2,1)S(1)}, bf16[1,1,128,128,128]{4,3,2,1,0:T(8,128)(2,1)}, u32[]{:S(2)}) copy-start(bf16[1,1,128,128,128]{4,3,2,1,0:T(8,128)(2,1)} %param.10) | copy-start | bytes 12582916
  49.3 33.8 %copy-start.2 = (bf16[512,512]{1,0:T(8,128)(2,1)S(1)}, bf16[512,512]{1,0:T(8,128)(2,1)}, u32[]{:S(2)}) copy-start(bf16[512,512]{1,0:T(8,128)(2,1)} %weight.1) | copy-start | bytes 1572868
  49.4 33.8 %copy-start.3 = (bf16[256,512]{1,0:T(8,128)(2,1)S(1)}, bf16[256,512]{1,0:T(8,128)(2,1)}, u32[]{:S(2)}) copy-start(bf16[256,512]{1,0:T(8,128)(2,1)} %cot.1) | copy-start | bytes 786436
  120.5 1.5 copy-start.4
  122.9 16.9 %all-to-all-start.3 = ((f32[8,64,256]{2,1,0:T(8,128)}), f32[8,64,256]{2,1,0:T(8,128)S(1)}, u32[]{:S(2)}, u32[]{:S(2)}) async-start(f32[8,64,256]{2,1,0:T(8,128)} %broadcast_in_dim.39), calls=%async_computation.3 | async-start | bytes 1048576 | tf_op jit(solution)/shard_map/all_to_all | solution.py:179
  128.8 2.8 %copy-start.1 = (bf16[1,1,128,128,128]{4,3,2,1,0:T(8,128)(2,1)S(1)}, bf16[1,1,128,128,128]{4,3,2,1,0:T(8,128)(2,1)}, u32[]{:S(2)}) copy-start(bf16[1,1,128,128,128]{4,3,2,1,0:T(8,128)(2,1)} %param.10) | copy-start | bytes 12582916
  139.8 51.9 %all-to-all-start.4 = ((bf16[16,256,256]{2,1,0:T(8,128)(2,1)}), bf16[16,256,256]{2,1,0:T(8,128)(2,1)S(1)}, u32[]{:S(2)}, u32[]{:S(2)}) async-start(bf16[16,256,256]{2,1,0:T(8,128)(2,1)} %bitcast.24), calls=%async_computation.4 | async-start | bytes 4194304 | tf_op jit(solution)/shard_map/all_to_all | solution.py:193
  150.4 1.3 collective-permute-start.2
  151.8 29.7 %collective-permute-start.3 = (f32[64,512]{1,0:T(8,128)S(1)}, f32[64,512]{1,0:T(8,128)}, u32[]{:S(2)}, u32[]{:S(2)}) collective-permute-start(f32[64,512]{1,0:T(8,128)S(1)} %maximum_select_fusion.1), channel_id=1, source_target_pairs={{0,16},{16,0},{32,48},{48,32},{64,80},{80,64},{96,112},{112,96},{1... | collective-permute-start | bytes 393224 | tf_op jit(solution)/shard_map/ppermute | solution.py:188
  151.9 31.6 %collective-permute-start.4 = (f32[64,512]{1,0:T(8,128)S(1)}, f32[64,512]{1,0:T(8,128)S(1)}, u32[]{:S(2)}, u32[]{:S(2)}) collective-permute-start(f32[64,512]{1,0:T(8,128)S(1)} %maximum_select_fusion.1), channel_id=1, source_target_pairs={{0,32},{16,48},{32,0},{48,16},{64,96},{80,112},{96,64},{112,80},{1... | collective-permute-start | bytes 393224 | tf_op jit(solution)/shard_map/ppermute | solution.py:188
  152.0 35.2 %collective-permute-start.5 = (f32[64,512]{1,0:T(8,128)S(1)}, f32[64,512]{1,0:T(8,128)S(1)}, u32[]{:S(2)}, u32[]{:S(2)}) collective-permute-start(f32[64,512]{1,0:T(8,128)S(1)} %maximum_select_fusion.1), channel_id=1, source_target_pairs={{0,48},{16,32},{32,16},{48,0},{64,112},{80,96},{96,80},{112,64},{1... | collective-permute-start | bytes 393224 | tf_op jit(solution)/shard_map/ppermute | solution.py:188
  154.5 32.7 %collective-permute-start.6 = (f32[64,512]{1,0:T(8,128)S(1)}, f32[64,512]{1,0:T(8,128)S(1)}, u32[]{:S(2)}, u32[]{:S(2)}) collective-permute-start(f32[64,512]{1,0:T(8,128)S(1)} %maximum_select_fusion.1), channel_id=1, source_target_pairs={{0,64},{16,80},{32,96},{48,112},{64,0},{80,16},{96,32},{112,48},{1... | collective-permute-start | bytes 393224 | tf_op jit(solution)/shard_map/ppermute | solution.py:188
  155.3 32.0 %collective-permute-start.7 = (f32[64,512]{1,0:T(8,128)S(1)}, f32[64,512]{1,0:T(8,128)S(1)}, u32[]{:S(2)}, u32[]{:S(2)}) collective-permute-start(f32[64,512]{1,0:T(8,128)S(1)} %maximum_select_fusion.1), channel_id=1, source_target_pairs={{0,80},{16,64},{32,112},{48,96},{64,16},{80,0},{96,48},{112,32},{1... | collective-permute-start | bytes 393224 | tf_op jit(solution)/shard_map/ppermute | solution.py:188
  181.5 5.8 %collective-permute-start.8 = (f32[64,512]{1,0:T(8,128)S(1)}, f32[64,512]{1,0:T(8,128)S(1)}, u32[]{:S(2)}, u32[]{:S(2)}) collective-permute-start(f32[64,512]{1,0:T(8,128)S(1)} %maximum_select_fusion.1), channel_id=1, source_target_pairs={{0,96},{16,112},{32,64},{48,80},{64,32},{80,48},{96,0},{112,16},{1... | collective-permute-start | bytes 393224 | tf_op jit(solution)/shard_map/ppermute | solution.py:188
  183.5 8.1 %collective-permute-start.9 = (f32[64,512]{1,0:T(8,128)S(1)}, f32[64,512]{1,0:T(8,128)S(1)}, u32[]{:S(2)}, u32[]{:S(2)}) collective-permute-start(f32[64,512]{1,0:T(8,128)S(1)} %maximum_select_fusion.1), channel_id=1, source_target_pairs={{0,112},{16,96},{32,80},{48,64},{64,48},{80,32},{96,16},{112,0},{1... | collective-permute-start | bytes 393224 | tf_op jit(solution)/shard_map/ppermute | solution.py:188
  191.7 1.3 copy-start.5

commit v3 on v1

v3 whole, which is shorter than its diff:
```python
import jax
import jax.numpy as jnp
from jax import lax
from jax.experimental import pallas as pl
from jax.experimental.pallas import tpu as pltpu
from jax.sharding import Mesh, PartitionSpec as P

BF = jnp.bfloat16
F32 = jnp.float32
CHUNK = 32
RING = 4
ROW = ("x", "zl", "core")
COL = ("y", "zh")
VMEM = pl.BlockSpec(memory_space=pltpu.VMEM)
SMEM = pl.BlockSpec(memory_space=pltpu.SMEM)
PARAMS = pltpu.CompilerParams(vmem_limit_bytes=40 << 20)


def tile_sums(forward, ids, own, sib, source, out_blocks):
    slots, side, _ = own.shape
    width = source.shape[-1]
    shape = (out_blocks, side, width)
    turns = slots // CHUNK

    def kernel(ids, own, sib, source, out, total, *fetched):
        def fetch(which, ref, turn):
            held, sems = fetched
            chunk = pl.ds(turn * CHUNK, CHUNK)
            return pltpu.make_async_copy(
                ref.at[chunk], held.at[which, chunk], sems.at[which * turns + turn]
            )

        if fetched:
            for which, ref in enumerate((own, sib)):
                for turn in range(turns):

                    @pl.when(ids[which, 2, 0] > turn * CHUNK)
                    def _(which=which, ref=ref, turn=turn):
                        fetch(which, ref, turn).start()

        total[...] = jnp.zeros_like(total)

        def block(index):
            return source[index // 2, pl.ds(pl.multiple_of(index % 2 * side, side), side)]

        for which, ref in enumerate((own, sib)):
            held = fetched[0].at[which] if fetched else ref

            def one(slot, which=which, held=held):
                r, c = ids[which, 0, slot], ids[which, 1, slot]
                if forward:
                    total[r] += jnp.dot(held[slot], block(c), preferred_element_type=F32)
                else:
                    total[c] += lax.dot_general(
                        held[slot], block(r), (((0,), (0,)), ((), ())), preferred_element_type=F32
                    )

            count = ids[which, 2, 0]

            @pl.loop(0, turns)
            def _(turn, which=which, ref=ref, one=one, count=count):
                start = turn * CHUNK
                if fetched:

                    @pl.when(count > start)
                    def _():
                        fetch(which, ref, turn).wait()

                @pl.when(count >= start + CHUNK)
                def _():
                    for u in range(CHUNK):
                        one(start + u)

                @pl.when((count > start) & (count < start + CHUNK))
                def _():
                    @pl.loop(start, count)
                    def _(slot):
                        one(slot)

        out[...] = total[...].astype(BF)

    scratch = [pltpu.VMEM(shape, F32)]
    if not forward:
        scratch += [
            pltpu.VMEM((2, slots, side, side), BF),
            pltpu.SemaphoreType.DMA((2 * turns,)),
        ]
    place = VMEM if forward else pl.BlockSpec(memory_space=pltpu.HBM)
    return pl.pallas_call(
        kernel,
        in_specs=[SMEM, place, place, VMEM],
        out_specs=VMEM,
        scratch_shapes=scratch,
        out_shape=jax.ShapeDtypeStruct(shape, BF),
        compiler_params=PARAMS if forward else pltpu.CompilerParams(vmem_limit_bytes=60 << 20),
        cost_estimate=pl.CostEstimate(
            flops=4 * slots * side * side * width, bytes_accessed=16 << 20, transcendentals=0
        ),
        name="forward_tiles" if forward else "backward_tiles",
    )(ids, own, sib, source)


def spread(features, cols):
    rows, width = features.shape
    half = width // 2

    def kernel(source, out):
        for s in range(2):
            piece = source[:, s * half : (s + 1) * half]
            for c in range(cols):
                out[s * cols + c] = piece

    return pl.pallas_call(
        kernel,
        in_specs=[VMEM],
        out_specs=VMEM,
        out_shape=jax.ShapeDtypeStruct((2 * cols, rows, half), BF),
        compiler_params=PARAMS,
        name="spread",
    )(features)


def finish(spot, parts, own, sibling):
    many, rows, half = parts.shape
    aways, pairs, _, share, _ = own.shape

    def kernel(spot, parts, own, sibling, out, wgrad):
        for s in range(2):
            here = slice(s * half, (s + 1) * half)
            total = parts[s * (many // 2)].astype(F32)
            for c in range(1, many // 2):
                total += parts[s * (many // 2) + c].astype(F32)
            out[:, here] = total.astype(BF)
            for d in range(aways):
                for q in range(pairs):
                    for other, ref in enumerate((own, sibling)):
                        r = ((spot[1] ^ d) * pairs + q) * 2 + (spot[0] ^ other)
                        at = pl.multiple_of(r * share, share)
                        wgrad[pl.ds(at, share), here] = ref[d, q, s].astype(F32)

    return pl.pallas_call(
        kernel,
        in_specs=[SMEM, VMEM, VMEM, VMEM],
        out_specs=(VMEM, VMEM),
        out_shape=(
            jax.ShapeDtypeStruct((rows, 2 * half), BF),
            jax.ShapeDtypeStruct((2 * half, 2 * half), F32),
        ),
        compiler_params=PARAMS,
        name="finish",
    )(spot, parts, own, sibling)


def middle(parts, weight, cotangent):
    many, own_rows, half = parts.shape
    chips = many // 2
    width = 2 * half
    share = width // many

    def kernel(parts, weight, cot, act, grad):
        w = weight[...]
        mixed = []
        for s in range(2):
            total = parts[s].astype(F32)
            for chip in range(1, chips):
                total += parts[chip * 2 + s].astype(F32)
            mixed.append(total.astype(BF))
        mixed = jnp.concatenate(mixed, axis=1)
        pre = jnp.dot(mixed, w, preferred_element_type=F32)
        sig = jax.nn.sigmoid(pre)
        act[...] = (pre * sig).astype(BF)
        slope = sig * (1.0 + pre * (1.0 - sig))
        grad_pre = (cot[...].astype(F32) * slope).astype(BF)
        wgrad = lax.dot_general(
            mixed, grad_pre, (((0,), (0,)), ((), ())), preferred_element_type=F32
        ).astype(BF)
        mixed_grad = lax.dot_general(
            grad_pre, w, (((1,), (1,)), ((), ())), preferred_element_type=F32
        ).astype(BF)
        for s in range(2):
            piece = mixed_grad[:, s * half : (s + 1) * half]
            for chip in range(chips):
                to = chip * 2 + s
                grad[to, :own_rows] = piece
                for h in range(2):
                    first = own_rows + h * share
                    grad[to, first : first + share] = wgrad[
                        to * share : (to + 1) * share, h * half : (h + 1) * half
                    ]

    return pl.pallas_call(
        kernel,
        in_specs=[VMEM, VMEM, VMEM],
        out_specs=(VMEM, VMEM),
        out_shape=(
            jax.ShapeDtypeStruct((own_rows, width), BF),
            jax.ShapeDtypeStruct((many, own_rows + 2 * share, half), BF),
        ),
        compiler_params=PARAMS,
        cost_estimate=pl.CostEstimate(
            flops=6 * own_rows * width * width, bytes_accessed=7 << 20, transcendentals=own_rows * width
        ),
        name="middle",
    )(parts, weight, cotangent)


def exchange(array, axes):
    return lax.all_to_all(array, axes, 0, 0, tiled=True)


def copies(array, count):
    return jnp.broadcast_to(array[None], (count, *array.shape))


def local(features, weight, cotangent, tiles, tile_rows, tile_cols, tile_count):
    slots, side = tiles.shape[2], tiles.shape[3]
    own_rows, width = features.shape
    chips = lax.axis_size(("x", "zl"))
    cols = lax.axis_size(COL)
    half = width // 2
    own_blocks = own_rows // side
    col_blocks = own_blocks * cols
    row_blocks = own_blocks * 2 * chips
    nodes = own_rows * 2 * chips * cols
    core = lax.axis_index("core")
    swap = [(0, 1), (1, 0)]

    ids = jnp.stack(
        [
            tile_rows[0, 0],
            tile_cols[0, 0] + core * col_blocks,
            jnp.broadcast_to(tile_count[0, 0], (slots,)),
        ]
    )
    ids = jnp.stack([ids, lax.ppermute(ids, "core", swap)])
    sent, ids, own = lax.optimization_barrier((spread(features, cols), ids, tiles))
    own = own[0, 0]
    sib = lax.ppermute(own, "core", swap)

    stripe = exchange(sent, ("core", *COL))
    sums = tile_sums(True, ids, own, sib, stripe, row_blocks)
    parts = exchange(sums.reshape(2 * chips, own_rows, half), ROW)
    act, grad = middle(parts, weight, cotangent)
    grad = exchange(grad, ROW)

    wgrad = grad[:, own_rows:].astype(F32).sum(0) * float(nodes) ** (-0.5)
    wgrad = exchange(copies(wgrad.astype(BF), 2 * cols), ("zl", *COL))
    back = tile_sums(False, ids, own, sib, grad, 2 * col_blocks)
    back, wgrad = lax.optimization_barrier((back, wgrad))
    wgrad = wgrad.reshape(2, cols, 2, -1, half).astype(F32).sum(1).astype(BF)
    wgrad = jnp.stack(
        [wgrad]
        + [lax.ppermute(wgrad, "x", [(i, i ^ d) for i in range(RING)]) for d in range(1, RING)]
    )
    sibling = lax.ppermute(wgrad, "core", swap)
    back = exchange(back.reshape(2 * cols, own_rows, half), ("core", *COL))
    spot = jnp.stack([core, lax.axis_index("x")])
    feature_grad, wgrad = finish(spot, back, wgrad, sibling)
    return act, wgrad, feature_grad


def solution(mesh):
    rows, cols = mesh.devices.shape
    fine = Mesh(
        mesh.devices.reshape(RING, rows // (2 * RING), 2, RING, cols // RING),
        ("x", "zl", "core", "y", "zh"),
    )
    in_specs = (
        P((*ROW, *COL), None),
        P(),
        P((*COL, *ROW), None),
        P(ROW, COL, None, None, None),
        P(ROW, COL, None),
        P(ROW, COL, None),
        P(ROW, COL, None),
    )
    out_specs = (P((*COL, *ROW), None), P(), P((*ROW, *COL), None))
    return jax.shard_map(local, mesh=fine, in_specs=in_specs, out_specs=out_specs, check_vma=False)
```

time: 307 us -> 175 us (0.57)
  waiting for transfers between devices: 199 us -> 25.8 us
  blocking collectives: 33.1 us -> 107 us
  between operations: 14.5 us -> 1.42 us
  local copies, waits for them, and re-layouts: 13 us -> 2.04 us
  starting transfers between devices: 26 us -> 21.4 us
    all_to_all x1 -> x3, blocking collectives: 33.1 us -> 107 us  [exchange(): return lax.all_to_all(array, axes, 0, 0, tiled=True)]
    psum x1 -> x0, waiting for transfers between devices: 69.7 us -> none  [local(): wgrad = lax.psum(wgrad, 'col') * float(nodes) ** (-0.5)]
    reduce_scatter x1 -> x0, waiting for transfers between devices: 64.1 us -> none  [local(): lax.psum_scatter(wgrad, ('chip', 'core'), scatter_dimension=0, tiled=True)]
    all_gather x1 -> x0, waiting for transfers between devices: 37.4 us -> none  [local(): wgrad = lax.all_gather(wgrad, ('chip', 'core'), axis=0, tiled=True)]
    unnamed x18 -> x14, local copies, waits for them, and re-layouts: 10.2 us -> 0.98 us
    all_to_all x3 -> x2, starting transfers between devices: 24.7 us -> 15.7 us  [exchange(): return lax.all_to_all(array, axes, 0, 0, tiled=True)]
    ppermute x1 -> x5, starting transfers between devices: 0.38 us -> 5.58 us  [the longest x3 3.32 us: local(): lax.ppermute(wgrad, 'x', [(i, i ^ d) for i in range(RING)])]
    all_to_all x3 -> x2, waiting for transfers between devices: 26.9 us -> 21.8 us  [exchange(): return lax.all_to_all(array, axes, 0, 0, tiled=True)]
  transfers between devices with their start and end apart: 8 -> 8, of which waited for: 5 -> 5; matrix products, arithmetic and copies ran while one was open for 2% -> 0% of each run, Pallas kernels for 2% -> 4%
where the time goes in v3:
time: 175 us; the launch traced here: 173 us
  blocking collectives  107 us (61%)
  waiting for transfers between devices  25.8 us (15%)
  starting transfers between devices  21.4 us (12%)
  Pallas kernels  14.1 us (8%)
  local copies, waits for them, and re-layouts  2.04 us (1%)
    all_to_all x3, blocking collectives, exchange(): return lax.all_to_all(array, axes, 0, 0, tiled=True)  107 us
    all_to_all x2, waiting for transfers between devices, exchange(): return lax.all_to_all(array, axes, 0, 0, tiled=True)  21.8 us
    all_to_all x2, starting transfers between devices, exchange(): return lax.all_to_all(array, axes, 0, 0, tiled=True)  15.7 us
    pallas_call x2, Pallas kernels, tile_sums(): pl.pallas_call(kernel, in_specs=[SMEM, place, place, VMEM], out_specs=VME...  10.6 us
  transfers between devices with their start and end apart: 8, of which 5 were waited for; matrix products, arithmetic and copies ran while one was open for 0% of the time, Pallas kernels for 4%

profile of v3, /device:TPU:17, one launch (start us, length us, event | category | flops | bytes accessed | tf_op | source)
XLA Modules:
  0.0 173.1 jit_solution(13943085830059882707)
XLA Ops:
  1.3 0.1 pad.10.clone
  1.4 0.7 add_bitcast_fusion
  2.0 0.7 fusion
  2.7 0.7 collective-permute-start
  3.4 0.0 copy-start.3
  3.4 0.9 copy-done.3
  4.4 0.1 spread.1
  4.5 0.0 collective-permute-done
  4.5 0.0 copy-start.5
  4.5 0.0 copy-start
  4.6 0.1 collective-permute-start.1
  4.6 34.8 %all_to_all.25.source = bf16[16,256,256]{2,1,0:T(8,128)(2,1)S(1)} all-to-all(bf16[16,256,256]{2,1,0:T(8,128)(2,1)S(1)} %spread.1), channel_id=1, replica_groups=mesh['x'=4,'zl'=2,'core'=2,'y'=4,'zh'=2] {'core','y','zh'}, dimensions={0} | all-to-all | bytes 4194304 | tf_op jit(solution)/shard_map/all_to_all | solution.py:208
  39.5 0.0 collective-permute-done.1.sib
  39.5 0.0 copy-done.5
  39.5 0.0 copy-done
  39.5 0.0 copy-start.1
  39.5 3.6 %forward_tiles.1 = bf16[32,128,256]{2,1,0:T(8,128)(2,1)S(1)} custom-call(s32[2,3,128]{2,1,0:T(4,128)S(1)} %pad_add_fusion.ids, bf16[128,128,128]{2,1,0:T(8,128)(2,1)S(1)} %bitcast.22, bf16[128,128,128]{2,1,0:T(8,128)(2,1)S(1)} %collective-permute-done.1.sib, bf16[16,256,256]{2,1,0:T(8,128)(2,1)S(1)} %all_to_all.25.source), custom_call_target="tpu_custom_call" | custom-call | flops 2147483648 | bytes 16777216 | tf_op jit(solution)/shard_map/forward_tiles/pallas_call | solution.py:89
  43.1 0.0 copy-done.1
  43.1 0.0 copy-start.2
  43.1 0.0 copy-start.4
  43.1 36.0 %all_to_all.26.parts = bf16[16,256,256]{2,1,0:T(8,128)(2,1)S(1)} all-to-all(bf16[16,256,256]{2,1,0:T(8,128)(2,1)S(1)} %bitcast.23), channel_id=1, replica_groups=mesh['x'=4,'zl'=2,'core'=2,'y'=4,'zh'=2] {'x','zl','core'}, dimensions={0} | all-to-all | bytes 4194304 | tf_op jit(solution)/shard_map/all_to_all | solution.py:208
  79.1 0.0 copy-done.2
  79.1 0.0 copy-done.4
  79.1 1.4 middle.1
  80.5 35.9 %all_to_all.27.source = bf16[16,320,256]{2,1,0:T(8,128)(2,1)S(1)} all-to-all(bf16[16,320,256]{2,1,0:T(8,128)(2,1)S(1)} %get-tuple-element.16), channel_id=1, replica_groups=mesh['x'=4,'zl'=2,'core'=2,'y'=4,'zh'=2] {'x','zl','core'}, dimensions={0} | all-to-all | bytes 5242880 | tf_op jit(solution)/shard_map/all_to_all | solution.py:208
  116.4 0.0 copy-start.6
  116.4 0.1 convert_reduce_fusion
  116.5 1.0 broadcast_in_dim.2
  117.5 5.4 %all-to-all-start.3 = ((bf16[16,64,256]{2,1,0:T(8,128)(2,1)}), bf16[16,64,256]{2,1,0:T(8,128)(2,1)S(1)}, u32[]{:S(2)}, u32[]{:S(2)}) async-start(bf16[16,64,256]{2,1,0:T(8,128)(2,1)} %broadcast_in_dim.2), calls=%async_computation.3 | async-start | bytes 1048576 | tf_op jit(solution)/shard_map/all_to_all | solution.py:208
  122.9 0.0 copy-done.6
  122.9 7.0 %backward_tiles.1 = bf16[32,128,256]{2,1,0:T(8,128)(2,1)} custom-call(s32[2,3,128]{2,1,0:T(4,128)} %copy-done.5, bf16[128,128,128]{2,1,0:T(8,128)(2,1)} %bitcast.21, bf16[128,128,128]{2,1,0:T(8,128)(2,1)} %copy-done.1, bf16[16,320,256]{2,1,0:T(8,128)(2,1)} %copy-done.6), custom_call_target="tpu_custom_call" | custom-call | flops 2147483648 | bytes 16777216 | tf_op jit(solution)/shard_map/backward_tiles/pallas_call | solution.py:89
  130.0 1.9 %all-to-all-done.3 = bf16[16,64,256]{2,1,0:T(8,128)(2,1)S(1)} async-done(((bf16[16,64,256]{2,1,0:T(8,128)(2,1)}), bf16[16,64,256]{2,1,0:T(8,128)(2,1)S(1)}, u32[]{:S(2)}, u32[]{:S(2)}) %all-to-all-start.3) | async-done | bytes 524320 | tf_op jit(solution)/shard_map/all_to_all | solution.py:208
  131.8 10.3 %all-to-all-start.4 = ((bf16[16,256,256]{2,1,0:T(8,128)(2,1)}), bf16[16,256,256]{2,1,0:T(8,128)(2,1)S(1)}, u32[]{:S(2)}, u32[]{:S(2)}) async-start(bf16[16,256,256]{2,1,0:T(8,128)(2,1)} %bitcast.24), calls=%async_computation.4 | async-start | bytes 4194304 | tf_op jit(solution)/shard_map/all_to_all | solution.py:208
  142.1 0.1 reduce_sum.22
  142.2 0.1 collective-permute-start.4
  142.3 0.1 collective-permute-start.3
  142.4 3.1 %collective-permute-start.2 = (bf16[2,2,32,256]{3,2,1,0:T(8,128)(2,1)S(1)}, bf16[2,2,32,256]{3,2,1,0:T(8,128)(2,1)S(1)}, u32[]{:S(2)}, u32[]{:S(2)}) collective-permute-start(bf16[2,2,32,256]{3,2,1,0:T(8,128)(2,1)S(1)} %reduce_sum.22), channel_id=1, source_target_pairs={{0,32},{32,0},{64,96},{96,64},{1,33},{33,1},{65,97},{97,65},{2,34}... | collective-permute-start | bytes 196616 | tf_op jit(solution)/shard_map/ppermute | solution.py:253
  145.5 2.7 %collective-permute-done.4 = bf16[2,2,32,256]{3,2,1,0:T(8,128)(2,1)S(1)} collective-permute-done((bf16[2,2,32,256]{3,2,1,0:T(8,128)(2,1)S(1)}, bf16[2,2,32,256]{3,2,1,0:T(8,128)(2,1)S(1)}, u32[]{:S(2)}, u32[]{:S(2)}) %collective-permute-start.4) | collective-permute-done | bytes 65568 | tf_op jit(solution)/shard_map/ppermute | solution.py:253
  148.3 0.0 collective-permute-done.3
  148.3 0.2 collective-permute-done.2
  148.5 1.6 collective-permute-start.5
  150.1 0.1 pad_add_fusion.1.spot
  150.2 1.1 collective-permute-done.5.sibling
  151.3 19.9 %all-to-all-done.4.parts = bf16[16,256,256]{2,1,0:T(8,128)(2,1)S(1)} async-done(((bf16[16,256,256]{2,1,0:T(8,128)(2,1)}), bf16[16,256,256]{2,1,0:T(8,128)(2,1)S(1)}, u32[]{:S(2)}, u32[]{:S(2)}) %all-to-all-start.4) | async-done | bytes 2097184 | tf_op jit(solution)/shard_map/all_to_all | solution.py:208
  171.2 1.9 %finish.1 = (bf16[256,512]{1,0:T(8,128)(2,1)}, f32[512,512]{1,0:T(8,128)}) custom-call(s32[2]{0:T(128)S(1)} %pad_add_fusion.1.spot, bf16[16,256,256]{2,1,0:T(8,128)(2,1)S(1)} %all-to-all-done.4.parts, bf16[4,2,2,32,256]{4,3,2,1,0:T(8,128)(2,1)S(1)} %pad_maximum_fusion.own, bf16[4,2,2,32,256]{4,3,2,1,0:T(8,128)(2,1)S(1)} %collective-permute-done.5.sibling), custom_call_target="tpu_custom_call" | custom-call | tf_op jit(solution)/shard_map/finish/pallas_call | solution.py:141
  (3 shorter events, 0.0 us)
Async XLA Ops:
  2.7 1.8 %collective-permute-start = (s32[3,128]{1,0:T(4,128)S(1)}, s32[3,128]{1,0:T(4,128)S(1)}, u32[]{:S(2)}, u32[]{:S(2)}) collective-permute-start(s32[3,128]{1,0:T(4,128)S(1)} %get-tuple-element.22), channel_id=1, source_target_pairs={{0,8},{8,0},{1,9},{9,1},{2,10},{10,2},{3,11},{11,3},{4,12},{12,4},... | collective-permute-start | bytes 4616 | tf_op jit(solution)/shard_map/ppermute | solution.py:235
  3.4 0.9 copy-start.3
  4.5 35.0 %copy-start.5 = (s32[2,3,128]{2,1,0:T(4,128)}, s32[2,3,128]{2,1,0:T(4,128)S(1)}, u32[]{:S(2)}) copy-start(s32[2,3,128]{2,1,0:T(4,128)S(1)} %pad_add_fusion.ids) | copy-start | bytes 9220
  4.5 35.0 %copy-start = (bf16[1,1,128,128,128]{4,3,2,1,0:T(8,128)(2,1)S(1)}, bf16[1,1,128,128,128]{4,3,2,1,0:T(8,128)(2,1)}, u32[]{:S(2)}) copy-start(bf16[1,1,128,128,128]{4,3,2,1,0:T(8,128)(2,1)} %param.10) | copy-start | bytes 12582916
  4.6 34.9 %collective-permute-start.1 = (bf16[128,128,128]{2,1,0:T(8,128)(2,1)}, bf16[128,128,128]{2,1,0:T(8,128)(2,1)S(1)}, u32[]{:S(2)}, u32[]{:S(2)}) collective-permute-start(bf16[128,128,128]{2,1,0:T(8,128)(2,1)} %bitcast.20), channel_id=1, source_target_pairs={{0,8},{8,0},{1,9},{9,1},{2,10},{10,2},{3,11},{11,3},{4,12},{12,4},... | collective-permute-start | bytes 12582920 | tf_op jit(solution)/shard_map/ppermute | solution.py:238
  39.5 3.6 %copy-start.1 = (bf16[128,128,128]{2,1,0:T(8,128)(2,1)}, bf16[128,128,128]{2,1,0:T(8,128)(2,1)S(1)}, u32[]{:S(2)}) copy-start(bf16[128,128,128]{2,1,0:T(8,128)(2,1)S(1)} %collective-permute-done.1.sib) | copy-start | bytes 12582916
  43.1 36.0 %copy-start.2 = (bf16[512,512]{1,0:T(8,128)(2,1)S(1)}, bf16[512,512]{1,0:T(8,128)(2,1)}, u32[]{:S(2)}) copy-start(bf16[512,512]{1,0:T(8,128)(2,1)} %weight.1) | copy-start | bytes 1572868
  43.1 36.0 %copy-start.4 = (bf16[256,512]{1,0:T(8,128)(2,1)S(1)}, bf16[256,512]{1,0:T(8,128)(2,1)}, u32[]{:S(2)}) copy-start(bf16[256,512]{1,0:T(8,128)(2,1)} %cot.1) | copy-start | bytes 786436
  116.4 6.5 %copy-start.6 = (bf16[16,320,256]{2,1,0:T(8,128)(2,1)}, bf16[16,320,256]{2,1,0:T(8,128)(2,1)S(1)}, u32[]{:S(2)}) copy-start(bf16[16,320,256]{2,1,0:T(8,128)(2,1)S(1)} %all_to_all.27.source) | copy-start | bytes 7864324
  117.5 14.3 %all-to-all-start.3 = ((bf16[16,64,256]{2,1,0:T(8,128)(2,1)}), bf16[16,64,256]{2,1,0:T(8,128)(2,1)S(1)}, u32[]{:S(2)}, u32[]{:S(2)}) async-start(bf16[16,64,256]{2,1,0:T(8,128)(2,1)} %broadcast_in_dim.2), calls=%async_computation.3 | async-start | bytes 1048576 | tf_op jit(solution)/shard_map/all_to_all | solution.py:208
  131.8 39.3 %all-to-all-start.4 = ((bf16[16,256,256]{2,1,0:T(8,128)(2,1)}), bf16[16,256,256]{2,1,0:T(8,128)(2,1)S(1)}, u32[]{:S(2)}, u32[]{:S(2)}) async-start(bf16[16,256,256]{2,1,0:T(8,128)(2,1)} %bitcast.24), calls=%async_computation.4 | async-start | bytes 4194304 | tf_op jit(solution)/shard_map/all_to_all | solution.py:208
  142.2 6.1 %collective-permute-start.4 = (bf16[2,2,32,256]{3,2,1,0:T(8,128)(2,1)S(1)}, bf16[2,2,32,256]{3,2,1,0:T(8,128)(2,1)S(1)}, u32[]{:S(2)}, u32[]{:S(2)}) collective-permute-start(bf16[2,2,32,256]{3,2,1,0:T(8,128)(2,1)S(1)} %reduce_sum.22), channel_id=1, source_target_pairs={{0,96},{32,64},{64,32},{96,0},{1,97},{33,65},{65,33},{97,1},{2,98}... | collective-permute-start | bytes 196616 | tf_op jit(solution)/shard_map/ppermute | solution.py:253
  142.3 6.0 %collective-permute-start.3 = (bf16[2,2,32,256]{3,2,1,0:T(8,128)(2,1)S(1)}, bf16[2,2,32,256]{3,2,1,0:T(8,128)(2,1)S(1)}, u32[]{:S(2)}, u32[]{:S(2)}) collective-permute-start(bf16[2,2,32,256]{3,2,1,0:T(8,128)(2,1)S(1)} %reduce_sum.22), channel_id=1, source_target_pairs={{0,64},{32,96},{64,0},{96,32},{1,65},{33,97},{65,1},{97,33},{2,66}... | collective-permute-start | bytes 196616 | tf_op jit(solution)/shard_map/ppermute | solution.py:253
  142.4 6.1 %collective-permute-start.2 = (bf16[2,2,32,256]{3,2,1,0:T(8,128)(2,1)S(1)}, bf16[2,2,32,256]{3,2,1,0:T(8,128)(2,1)S(1)}, u32[]{:S(2)}, u32[]{:S(2)}) collective-permute-start(bf16[2,2,32,256]{3,2,1,0:T(8,128)(2,1)S(1)} %reduce_sum.22), channel_id=1, source_target_pairs={{0,32},{32,0},{64,96},{96,64},{1,33},{33,1},{65,97},{97,65},{2,34}... | collective-permute-start | bytes 196616 | tf_op jit(solution)/shard_map/ppermute | solution.py:253
  148.5 2.8 %collective-permute-start.5 = (bf16[4,2,2,32,256]{4,3,2,1,0:T(8,128)(2,1)S(1)}, bf16[4,2,2,32,256]{4,3,2,1,0:T(8,128)(2,1)S(1)}, u32[]{:S(2)}, u32[]{:S(2)}) collective-permute-start(bf16[4,2,2,32,256]{4,3,2,1,0:T(8,128)(2,1)S(1)} %pad_maximum_fusion.own), channel_id=1, source_target_pairs={{0,8},{8,0},{1,9},{9,1},{2,10},{10,2},{3,11},{11,3},{4,12},{12,4},... | collective-permute-start | bytes 786440 | tf_op jit(solution)/shard_map/ppermute | solution.py:255

commit v4 on v3

--- a/solution.py
+++ b/solution.py
@@ -20,31 +20,14 @@
     slots, side, _ = own.shape
     width = source.shape[-1]
     shape = (out_blocks, side, width)
-    turns = slots // CHUNK
-
-    def kernel(ids, own, sib, source, out, total, *fetched):
-        def fetch(which, ref, turn):
-            held, sems = fetched
-            chunk = pl.ds(turn * CHUNK, CHUNK)
-            return pltpu.make_async_copy(
-                ref.at[chunk], held.at[which, chunk], sems.at[which * turns + turn]
-            )
-
-        if fetched:
-            for which, ref in enumerate((own, sib)):
-                for turn in range(turns):
-
-                    @pl.when(ids[which, 2, 0] > turn * CHUNK)
-                    def _(which=which, ref=ref, turn=turn):
-                        fetch(which, ref, turn).start()
-
+
+    def kernel(ids, own, sib, source, out, total):
         total[...] = jnp.zeros_like(total)
 
         def block(index):
             return source[index // 2, pl.ds(pl.multiple_of(index % 2 * side, side), side)]
 
-        for which, ref in enumerate((own, sib)):
-            held = fetched[0].at[which] if fetched else ref
+        for which, held in enumerate((own, sib)):
 
             def one(slot, which=which, held=held):
                 r, c = ids[which, 0, slot], ids[which, 1, slot]
@@ -57,14 +40,9 @@
 
             count = ids[which, 2, 0]
 
-            @pl.loop(0, turns)
-            def _(turn, which=which, ref=ref, one=one, count=count):
+            @pl.loop(0, slots // CHUNK)
+            def _(turn, one=one, count=count):
                 start = turn * CHUNK
-                if fetched:
-
-                    @pl.when(count > start)
-                    def _():
-                        fetch(which, ref, turn).wait()
 
                 @pl.when(count >= start + CHUNK)
                 def _():
@@ -79,20 +57,13 @@
 
         out[...] = total[...].astype(BF)
 
-    scratch = [pltpu.VMEM(shape, F32)]
-    if not forward:
-        scratch += [
-            pltpu.VMEM((2, slots, side, side), BF),
-            pltpu.SemaphoreType.DMA((2 * turns,)),
-        ]
-    place = VMEM if forward else pl.BlockSpec(memory_space=pltpu.HBM)
-    return pl.pallas_call(
-        kernel,
-        in_specs=[SMEM, place, place, VMEM],
-        out_specs=VMEM,
-        scratch_shapes=scratch,
+    return pl.pallas_call(
+        kernel,
+        in_specs=[SMEM, VMEM, VMEM, VMEM],
+        out_specs=VMEM,
+        scratch_shapes=[pltpu.VMEM(shape, F32)],
         out_shape=jax.ShapeDtypeStruct(shape, BF),
-        compiler_params=PARAMS if forward else pltpu.CompilerParams(vmem_limit_bytes=60 << 20),
+        compiler_params=PARAMS,
         cost_estimate=pl.CostEstimate(
             flops=4 * slots * side * side * width, bytes_accessed=16 << 20, transcendentals=0
         ),
@@ -120,35 +91,48 @@
     )(features)
 
 
-def finish(spot, parts, own, sibling):
+def column_sum(parts):
     many, rows, half = parts.shape
-    aways, pairs, _, share, _ = own.shape
-
-    def kernel(spot, parts, own, sibling, out, wgrad):
-        for s in range(2):
-            here = slice(s * half, (s + 1) * half)
+
+    def kernel(parts, out):
+        for s in range(2):
             total = parts[s * (many // 2)].astype(F32)
             for c in range(1, many // 2):
                 total += parts[s * (many // 2) + c].astype(F32)
-            out[:, here] = total.astype(BF)
+            out[:, s * half : (s + 1) * half] = total.astype(BF)
+
+    return pl.pallas_call(
+        kernel,
+        in_specs=[VMEM],
+        out_specs=VMEM,
+        out_shape=jax.ShapeDtypeStruct((rows, 2 * half), BF),
+        compiler_params=PARAMS,
+        name="column_sum",
+    )(parts)
+
+
+def place_shares(spot, own, sibling):
+    aways, pairs, _, share, half = own.shape
+
+    def kernel(spot, own, sibling, wgrad):
+        for s in range(2):
+            here = slice(s * half, (s + 1) * half)
             for d in range(aways):
                 for q in range(pairs):
                     for other, ref in enumerate((own, sibling)):
-                        r = ((spot[1] ^ d) * pairs + q) * 2 + (spot[0] ^ other)
+                        r = ((spot[1] ^ d) * pairs + (spot[2] ^ q)) * 2 + (spot[0] ^ other)
                         at = pl.multiple_of(r * share, share)
                         wgrad[pl.ds(at, share), here] = ref[d, q, s].astype(F32)
 
     return pl.pallas_call(
         kernel,
-        in_specs=[SMEM, VMEM, VMEM, VMEM],
-        out_specs=(VMEM, VMEM),
-        out_shape=(
-            jax.ShapeDtypeStruct((rows, 2 * half), BF),
-            jax.ShapeDtypeStruct((2 * half, 2 * half), F32),
-        ),
-        compiler_params=PARAMS,
-        name="finish",
-    )(spot, parts, own, sibling)
+        in_specs=[SMEM, VMEM, VMEM],
+        out_specs=VMEM,
+        out_shape=jax.ShapeDtypeStruct((2 * half, 2 * half), F32),
+        compiler_params=PARAMS,
+        cost_estimate=pl.CostEstimate(flops=0, bytes_accessed=2 << 20, transcendentals=0),
+        name="place_shares",
+    )(spot, own, sibling)
 
 
 def middle(parts, weight, cotangent):
@@ -204,6 +188,11 @@
     )(parts, weight, cotangent)
 
 
+def flip(array, axis, by=1):
+    size = RING if axis in ("x", "y") else 2
+    return lax.ppermute(array, axis, [(i, i ^ by) for i in range(size)])
+
+
 def exchange(array, axes):
     return lax.all_to_all(array, axes, 0, 0, tiled=True)
 
@@ -244,19 +233,18 @@
     grad = exchange(grad, ROW)
 
     wgrad = grad[:, own_rows:].astype(F32).sum(0) * float(nodes) ** (-0.5)
-    wgrad = exchange(copies(wgrad.astype(BF), 2 * cols), ("zl", *COL))
+    near, *far = (flip(wgrad, "y", d) for d in range(1, RING))
     back = tile_sums(False, ids, own, sib, grad, 2 * col_blocks)
-    back, wgrad = lax.optimization_barrier((back, wgrad))
-    wgrad = wgrad.reshape(2, cols, 2, -1, half).astype(F32).sum(1).astype(BF)
-    wgrad = jnp.stack(
-        [wgrad]
-        + [lax.ppermute(wgrad, "x", [(i, i ^ d) for i in range(RING)]) for d in range(1, RING)]
-    )
-    sibling = lax.ppermute(wgrad, "core", swap)
+    back, near, far = lax.optimization_barrier((back, near, far))
+    wgrad = (wgrad + near) + (far[0] + far[1])
+    across = lax.ppermute(wgrad, ("zl", "zh"), [(i, 3 - i) for i in range(4)])
+    wgrad = jnp.stack([wgrad + flip(wgrad, "zh"), flip(wgrad, "zl") + across])
+    wgrad = wgrad.reshape(2, 2, -1, half).astype(BF)
+    wgrad = jnp.stack([wgrad, *(flip(wgrad, "x", d) for d in range(1, RING))])
+    sibling = flip(wgrad, "core")
     back = exchange(back.reshape(2 * cols, own_rows, half), ("core", *COL))
-    spot = jnp.stack([core, lax.axis_index("x")])
-    feature_grad, wgrad = finish(spot, back, wgrad, sibling)
-    return act, wgrad, feature_grad
+    spot = jnp.stack([core, lax.axis_index("x"), lax.axis_index("zl")])
+    return act, place_shares(spot, wgrad, sibling), column_sum(back)
 
 
 def solution(mesh):

time: 175 us -> 171 us (0.977)
  starting transfers between devices: 21.4 us -> 32.7 us
  waiting for transfers between devices: 25.8 us -> 15 us
  blocking collectives: 107 us -> 103 us
    all_to_all x2 -> x1, waiting for transfers between devices: 21.8 us -> 0.01 us  [exchange(): return lax.all_to_all(array, axes, 0, 0, tiled=True)]
    ppermute x4 -> x10, starting transfers between devices: 4.91 us -> 23.3 us  [the longest x9 23.3 us: flip(): return lax.ppermute(array, axis, [(i, i ^ by) for i in range(size)])]
    ppermute x4 -> x10, waiting for transfers between devices: 4.02 us -> 15 us  [the longest x9 12.9 us: flip(): return lax.ppermute(array, axis, [(i, i ^ by) for i in range(size)])]
    all_to_all x2 -> x1, starting transfers between devices: 15.7 us -> 8.66 us  [exchange(): return lax.all_to_all(array, axes, 0, 0, tiled=True)]
    all_to_all x3, blocking collectives: 107 us -> 103 us  [exchange(): return lax.all_to_all(array, axes, 0, 0, tiled=True)]
    pallas_call x3 -> x4, Pallas kernels: 12.5 us -> 12.6 us  [the longest x2 10.1 us: tile_sums(): pl.pallas_call(kernel, in_specs=[SMEM, VMEM, VMEM, VMEM], out_specs=VMEM,...]
  transfers between devices with their start and end apart: 8 -> 13, of which waited for: 5 -> 5; matrix products, arithmetic and copies ran while one was open for 0% -> 0% of each run, Pallas kernels for 4% -> 4%
where the time goes in v4:
time: 171 us; the launch traced here: 170 us
  blocking collectives  103 us (60%)
  starting transfers between devices  32.7 us (19%)
  waiting for transfers between devices  15 us (9%)
  Pallas kernels  14.1 us (8%)
  local copies, waits for them, and re-layouts  2.37 us (1%)
    all_to_all x3, blocking collectives, exchange(): return lax.all_to_all(array, axes, 0, 0, tiled=True)  103 us
    ppermute x9, starting transfers between devices, flip(): return lax.ppermute(array, axis, [(i, i ^ by) for i in range(size)])  23.3 us
    ppermute x9, waiting for transfers between devices, flip(): return lax.ppermute(array, axis, [(i, i ^ by) for i in range(size)])  12.9 us
    pallas_call x2, Pallas kernels, tile_sums(): pl.pallas_call(kernel, in_specs=[SMEM, VMEM, VMEM, VMEM], out_specs=VMEM,...  10.1 us
    all_to_all x1, starting transfers between devices, exchange(): return lax.all_to_all(array, axes, 0, 0, tiled=True)  8.66 us
  transfers between devices with their start and end apart: 13, of which 5 were waited for; matrix products, arithmetic and copies ran while one was open for 0% of the time, Pallas kernels for 4%

profile of v4, /device:TPU:17, one launch (start us, length us, event | category | flops | bytes accessed | tf_op | source)
XLA Modules:
  0.0 169.9 jit_solution(6972784801448222667)
XLA Ops:
  1.3 0.1 pad.14.clone
  1.4 0.7 add_bitcast_fusion
  2.0 0.7 fusion
  2.7 0.7 collective-permute-start
  3.4 0.9 copy-done.3
  4.4 0.1 spread.1
  4.5 0.0 collective-permute-done
  4.5 0.0 copy-start
  4.5 0.1 collective-permute-start.1
  4.6 34.8 %all_to_all.20.source = bf16[16,256,256]{2,1,0:T(8,128)(2,1)S(1)} all-to-all(bf16[16,256,256]{2,1,0:T(8,128)(2,1)S(1)} %spread.1), channel_id=1, replica_groups=mesh['x'=4,'zl'=2,'core'=2,'y'=4,'zh'=2] {'core','y','zh'}, dimensions={0} | all-to-all | bytes 4194304 | tf_op jit(solution)/shard_map/all_to_all | solution.py:197
  39.5 0.0 collective-permute-done.1.sib
  39.5 0.0 copy-done
  39.5 5.1 %forward_tiles.1 = bf16[32,128,256]{2,1,0:T(8,128)(2,1)S(1)} custom-call(s32[2,3,128]{2,1,0:T(4,128)S(1)} %pad_add_fusion.ids, bf16[128,128,128]{2,1,0:T(8,128)(2,1)S(1)} %bitcast.24, bf16[128,128,128]{2,1,0:T(8,128)(2,1)S(1)} %collective-permute-done.1.sib, bf16[16,256,256]{2,1,0:T(8,128)(2,1)S(1)} %all_to_all.20.source), custom_call_target="tpu_custom_call" | custom-call | flops 2147483648 | bytes 16777216 | tf_op jit(solution)/shard_map/forward_tiles/pallas_call | solution.py:60
  44.5 0.0 copy-start.2
  44.6 0.0 copy-start.4
  44.6 32.0 %all_to_all.21.parts = bf16[16,256,256]{2,1,0:T(8,128)(2,1)S(1)} all-to-all(bf16[16,256,256]{2,1,0:T(8,128)(2,1)S(1)} %bitcast.27), channel_id=1, replica_groups=mesh['x'=4,'zl'=2,'core'=2,'y'=4,'zh'=2] {'x','zl','core'}, dimensions={0} | all-to-all | bytes 4194304 | tf_op jit(solution)/shard_map/all_to_all | solution.py:197
  76.5 0.0 copy-done.2
  76.5 0.0 copy-done.4
  76.5 1.4 middle.1
  77.9 35.9 %all_to_all.22.source = bf16[16,320,256]{2,1,0:T(8,128)(2,1)S(1)} all-to-all(bf16[16,320,256]{2,1,0:T(8,128)(2,1)S(1)} %get-tuple-element.16), channel_id=1, replica_groups=mesh['x'=4,'zl'=2,'core'=2,'y'=4,'zh'=2] {'x','zl','core'}, dimensions={0} | all-to-all | bytes 5242880 | tf_op jit(solution)/shard_map/all_to_all | solution.py:197
  113.9 0.1 convert_reduce_fusion
  114.0 2.9 %collective-permute-start.4 = (f32[64,256]{1,0:T(8,128)S(1)}, f32[64,256]{1,0:T(8,128)S(1)}, u32[]{:S(2)}, u32[]{:S(2)}) collective-permute-start(f32[64,256]{1,0:T(8,128)S(1)} %broadcast_multiply_fusion), channel_id=1, source_target_pairs={{0,6},{2,4},{4,2},{6,0},{1,7},{3,5},{5,3},{7,1},{8,14},{10,12},{12... | collective-permute-start | bytes 196616 | tf_op jit(solution)/shard_map/ppermute | solution.py:193
  116.8 1.4 collective-permute-start.3
  118.2 0.5 collective-permute-start.2
  118.7 5.0 %backward_tiles.1 = bf16[32,128,256]{2,1,0:T(8,128)(2,1)S(1)} custom-call(s32[2,3,128]{2,1,0:T(4,128)S(1)} %pad_add_fusion.ids, bf16[128,128,128]{2,1,0:T(8,128)(2,1)S(1)} %bitcast.25, bf16[128,128,128]{2,1,0:T(8,128)(2,1)S(1)} %collective-permute-done.1.sib, bf16[16,320,256]{2,1,0:T(8,128)(2,1)S(1)} %all_to_all.22.source), custom_call_target="tpu_custom_call" | custom-call | flops 2147483648 | bytes 16777216 | tf_op jit(solution)/shard_map/backward_tiles/pallas_call | solution.py:60
  123.7 1.3 copy-done.1
  125.0 0.0 collective-permute-done.4
  125.0 0.0 collective-permute-done.3
  125.0 0.0 collective-permute-done.2
  125.1 8.7 %all-to-all-start.3 = ((bf16[16,256,256]{2,1,0:T(8,128)(2,1)}), bf16[16,256,256]{2,1,0:T(8,128)(2,1)S(1)}, u32[]{:S(2)}, u32[]{:S(2)}) async-start(bf16[16,256,256]{2,1,0:T(8,128)(2,1)} %bitcast.26), calls=%async_computation.3 | async-start | bytes 4194304 | tf_op jit(solution)/shard_map/all_to_all | solution.py:197
  133.7 2.8 %collective-permute-start.5 = (f32[64,256]{1,0:T(8,128)S(1)}, f32[64,256]{1,0:T(8,128)S(1)}, u32[]{:S(2)}, u32[]{:S(2)}) collective-permute-start(f32[64,256]{1,0:T(8,128)S(1)} %add_add_fusion), channel_id=1, source_target_pairs={{0,1},{1,0},{2,3},{3,2},{4,5},{5,4},{6,7},{7,6},{8,9},{9,8},{10,11... | collective-permute-start | bytes 196616 | tf_op jit(solution)/shard_map/ppermute | solution.py:193
  136.5 0.0 collective-permute-start.7
  136.5 0.0 collective-permute-start.6
  136.5 8.1 %collective-permute-done.5 = f32[64,256]{1,0:T(8,128)S(1)} collective-permute-done((f32[64,256]{1,0:T(8,128)S(1)}, f32[64,256]{1,0:T(8,128)S(1)}, u32[]{:S(2)}, u32[]{:S(2)}) %collective-permute-start.5) | collective-permute-done | bytes 65568 | tf_op jit(solution)/shard_map/ppermute | solution.py:193
  144.6 2.1 %collective-permute-done.7 = f32[64,256]{1,0:T(8,128)S(1)} collective-permute-done((f32[64,256]{1,0:T(8,128)S(1)}, f32[64,256]{1,0:T(8,128)S(1)}, u32[]{:S(2)}, u32[]{:S(2)}) %collective-permute-start.7) | collective-permute-done | bytes 65568 | tf_op jit(solution)/shard_map/ppermute | solution.py:240
  146.6 0.0 collective-permute-done.6
  146.7 2.2 %collective-permute-start.10 = (bf16[2,2,32,256]{3,2,1,0:T(8,128)(2,1)S(1)}, bf16[2,2,32,256]{3,2,1,0:T(8,128)(2,1)S(1)}, u32[]{:S(2)}, u32[]{:S(2)}) collective-permute-start(bf16[2,2,32,256]{3,2,1,0:T(8,128)(2,1)S(1)} %pad_maximum_fusion.1), channel_id=1, source_target_pairs={{0,96},{32,64},{64,32},{96,0},{1,97},{33,65},{65,33},{97,1},{2,98}... | collective-permute-start | bytes 196616 | tf_op jit(solution)/shard_map/ppermute | solution.py:193
  148.8 0.4 collective-permute-start.9
  149.2 0.8 collective-permute-start.8
  150.0 1.4 collective-permute-done.10
  151.4 2.4 %collective-permute-done.9 = bf16[2,2,32,256]{3,2,1,0:T(8,128)(2,1)S(1)} collective-permute-done((bf16[2,2,32,256]{3,2,1,0:T(8,128)(2,1)S(1)}, bf16[2,2,32,256]{3,2,1,0:T(8,128)(2,1)S(1)}, u32[]{:S(2)}, u32[]{:S(2)}) %collective-permute-start.9) | collective-permute-done | bytes 65568 | tf_op jit(solution)/shard_map/ppermute | solution.py:193
  153.7 0.0 collective-permute-done.8
  153.8 12.4 %collective-permute-start.11 = (bf16[4,2,2,32,256]{4,3,2,1,0:T(8,128)(2,1)S(1)}, bf16[4,2,2,32,256]{4,3,2,1,0:T(8,128)(2,1)S(1)}, u32[]{:S(2)}, u32[]{:S(2)}) collective-permute-start(bf16[4,2,2,32,256]{4,3,2,1,0:T(8,128)(2,1)S(1)} %pad_maximum_fusion.own), channel_id=1, source_target_pairs={{0,8},{8,0},{1,9},{9,1},{2,10},{10,2},{3,11},{11,3},{4,12},{12,4},... | collective-permute-start | bytes 786440 | tf_op jit(solution)/shard_map/ppermute | solution.py:193
  166.2 0.1 pad_add_fusion.1.spot
  166.3 1.1 collective-permute-done.11.sibling
  167.4 1.6 place_shares.1
  169.0 0.0 all-to-all-done.3.parts
  169.0 1.0 column_sum.1
  (9 shorter events, 0.1 us)
Async XLA Ops:
  2.7 1.8 %collective-permute-start = (s32[3,128]{1,0:T(4,128)S(1)}, s32[3,128]{1,0:T(4,128)S(1)}, u32[]{:S(2)}, u32[]{:S(2)}) collective-permute-start(s32[3,128]{1,0:T(4,128)S(1)} %get-tuple-element.22), channel_id=1, source_target_pairs={{0,8},{8,0},{1,9},{9,1},{2,10},{10,2},{3,11},{11,3},{4,12},{12,4},... | collective-permute-start | bytes 4616 | tf_op jit(solution)/shard_map/ppermute | solution.py:224
  3.4 0.9 copy-start.3
  4.5 35.0 %copy-start = (bf16[1,1,128,128,128]{4,3,2,1,0:T(8,128)(2,1)S(1)}, bf16[1,1,128,128,128]{4,3,2,1,0:T(8,128)(2,1)}, u32[]{:S(2)}) copy-start(bf16[1,1,128,128,128]{4,3,2,1,0:T(8,128)(2,1)} %param.10) | copy-start | bytes 12582916
  4.5 34.9 %collective-permute-start.1 = (bf16[128,128,128]{2,1,0:T(8,128)(2,1)}, bf16[128,128,128]{2,1,0:T(8,128)(2,1)S(1)}, u32[]{:S(2)}, u32[]{:S(2)}) collective-permute-start(bf16[128,128,128]{2,1,0:T(8,128)(2,1)} %bitcast.23), channel_id=1, source_target_pairs={{0,8},{8,0},{1,9},{9,1},{2,10},{10,2},{3,11},{11,3},{4,12},{12,4},... | collective-permute-start | bytes 12582920 | tf_op jit(solution)/shard_map/ppermute | solution.py:227
  44.5 32.0 %copy-start.2 = (bf16[512,512]{1,0:T(8,128)(2,1)S(1)}, bf16[512,512]{1,0:T(8,128)(2,1)}, u32[]{:S(2)}) copy-start(bf16[512,512]{1,0:T(8,128)(2,1)} %weight.1) | copy-start | bytes 1572868
  44.6 32.0 %copy-start.4 = (bf16[256,512]{1,0:T(8,128)(2,1)S(1)}, bf16[256,512]{1,0:T(8,128)(2,1)}, u32[]{:S(2)}) copy-start(bf16[256,512]{1,0:T(8,128)(2,1)} %cot.1) | copy-start | bytes 786436
  114.0 11.1 %collective-permute-start.4 = (f32[64,256]{1,0:T(8,128)S(1)}, f32[64,256]{1,0:T(8,128)S(1)}, u32[]{:S(2)}, u32[]{:S(2)}) collective-permute-start(f32[64,256]{1,0:T(8,128)S(1)} %broadcast_multiply_fusion), channel_id=1, source_target_pairs={{0,6},{2,4},{4,2},{6,0},{1,7},{3,5},{5,3},{7,1},{8,14},{10,12},{12... | collective-permute-start | bytes 196616 | tf_op jit(solution)/shard_map/ppermute | solution.py:193
  116.8 8.2 %collective-permute-start.3 = (f32[64,256]{1,0:T(8,128)S(1)}, f32[64,256]{1,0:T(8,128)S(1)}, u32[]{:S(2)}, u32[]{:S(2)}) collective-permute-start(f32[64,256]{1,0:T(8,128)S(1)} %broadcast_multiply_fusion), channel_id=1, source_target_pairs={{0,4},{2,6},{4,0},{6,2},{1,5},{3,7},{5,1},{7,3},{8,12},{10,14},{12... | collective-permute-start | bytes 196616 | tf_op jit(solution)/shard_map/ppermute | solution.py:193
  118.2 6.8 %collective-permute-start.2 = (f32[64,256]{1,0:T(8,128)S(1)}, f32[64,256]{1,0:T(8,128)S(1)}, u32[]{:S(2)}, u32[]{:S(2)}) collective-permute-start(f32[64,256]{1,0:T(8,128)S(1)} %broadcast_multiply_fusion), channel_id=1, source_target_pairs={{0,2},{2,0},{4,6},{6,4},{1,3},{3,1},{5,7},{7,5},{8,10},{10,8},{12,... | collective-permute-start | bytes 196616 | tf_op jit(solution)/shard_map/ppermute | solution.py:193
  123.7 1.3 copy-start.1
  125.1 43.9 %all-to-all-start.3 = ((bf16[16,256,256]{2,1,0:T(8,128)(2,1)}), bf16[16,256,256]{2,1,0:T(8,128)(2,1)S(1)}, u32[]{:S(2)}, u32[]{:S(2)}) async-start(bf16[16,256,256]{2,1,0:T(8,128)(2,1)} %bitcast.26), calls=%async_computation.3 | async-start | bytes 4194304 | tf_op jit(solution)/shard_map/all_to_all | solution.py:197
  133.7 10.8 %collective-permute-start.5 = (f32[64,256]{1,0:T(8,128)S(1)}, f32[64,256]{1,0:T(8,128)S(1)}, u32[]{:S(2)}, u32[]{:S(2)}) collective-permute-start(f32[64,256]{1,0:T(8,128)S(1)} %add_add_fusion), channel_id=1, source_target_pairs={{0,1},{1,0},{2,3},{3,2},{4,5},{5,4},{6,7},{7,6},{8,9},{9,8},{10,11... | collective-permute-start | bytes 196616 | tf_op jit(solution)/shard_map/ppermute | solution.py:193
  136.5 10.1 %collective-permute-start.7 = (f32[64,256]{1,0:T(8,128)S(1)}, f32[64,256]{1,0:T(8,128)S(1)}, u32[]{:S(2)}, u32[]{:S(2)}) collective-permute-start(f32[64,256]{1,0:T(8,128)S(1)} %add_add_fusion), channel_id=1, source_target_pairs={{0,17},{1,16},{16,1},{17,0},{2,19},{3,18},{18,3},{19,2},{4,21},{5,... | collective-permute-start | bytes 196616 | tf_op jit(solution)/shard_map/ppermute | solution.py:240
  136.5 10.1 %collective-permute-start.6 = (f32[64,256]{1,0:T(8,128)S(1)}, f32[64,256]{1,0:T(8,128)S(1)}, u32[]{:S(2)}, u32[]{:S(2)}) collective-permute-start(f32[64,256]{1,0:T(8,128)S(1)} %add_add_fusion), channel_id=1, source_target_pairs={{0,16},{16,0},{1,17},{17,1},{2,18},{18,2},{3,19},{19,3},{4,20},{20... | collective-permute-start | bytes 196616 | tf_op jit(solution)/shard_map/ppermute | solution.py:193
  146.7 4.7 %collective-permute-start.10 = (bf16[2,2,32,256]{3,2,1,0:T(8,128)(2,1)S(1)}, bf16[2,2,32,256]{3,2,1,0:T(8,128)(2,1)S(1)}, u32[]{:S(2)}, u32[]{:S(2)}) collective-permute-start(bf16[2,2,32,256]{3,2,1,0:T(8,128)(2,1)S(1)} %pad_maximum_fusion.1), channel_id=1, source_target_pairs={{0,96},{32,64},{64,32},{96,0},{1,97},{33,65},{65,33},{97,1},{2,98}... | collective-permute-start | bytes 196616 | tf_op jit(solution)/shard_map/ppermute | solution.py:193
  148.8 4.9 %collective-permute-start.9 = (bf16[2,2,32,256]{3,2,1,0:T(8,128)(2,1)S(1)}, bf16[2,2,32,256]{3,2,1,0:T(8,128)(2,1)S(1)}, u32[]{:S(2)}, u32[]{:S(2)}) collective-permute-start(bf16[2,2,32,256]{3,2,1,0:T(8,128)(2,1)S(1)} %pad_maximum_fusion.1), channel_id=1, source_target_pairs={{0,64},{32,96},{64,0},{96,32},{1,65},{33,97},{65,1},{97,33},{2,66}... | collective-permute-start | bytes 196616 | tf_op jit(solution)/shard_map/ppermute | solution.py:193
  149.2 4.5 %collective-permute-start.8 = (bf16[2,2,32,256]{3,2,1,0:T(8,128)(2,1)S(1)}, bf16[2,2,32,256]{3,2,1,0:T(8,128)(2,1)S(1)}, u32[]{:S(2)}, u32[]{:S(2)}) collective-permute-start(bf16[2,2,32,256]{3,2,1,0:T(8,128)(2,1)S(1)} %pad_maximum_fusion.1), channel_id=1, source_target_pairs={{0,32},{32,0},{64,96},{96,64},{1,33},{33,1},{65,97},{97,65},{2,34}... | collective-permute-start | bytes 196616 | tf_op jit(solution)/shard_map/ppermute | solution.py:193
  153.8 13.6 %collective-permute-start.11 = (bf16[4,2,2,32,256]{4,3,2,1,0:T(8,128)(2,1)S(1)}, bf16[4,2,2,32,256]{4,3,2,1,0:T(8,128)(2,1)S(1)}, u32[]{:S(2)}, u32[]{:S(2)}) collective-permute-start(bf16[4,2,2,32,256]{4,3,2,1,0:T(8,128)(2,1)S(1)} %pad_maximum_fusion.own), channel_id=1, source_target_pairs={{0,8},{8,0},{1,9},{9,1},{2,10},{10,2},{3,11},{11,3},{4,12},{12,4},... | collective-permute-start | bytes 786440 | tf_op jit(solution)/shard_map/ppermute | solution.py:193

commit v5 on v4

--- a/solution.py
+++ b/solution.py
@@ -7,10 +7,12 @@
 
 BF = jnp.bfloat16
 F32 = jnp.float32
-CHUNK = 32
+SIZES = (64, 16, 1)
 RING = 4
 ROW = ("x", "zl", "core")
 COL = ("y", "zh")
+ROW_ORDER = ("zl", "x", "core")
+COL_ORDER = ("zh", "y", "core")
 VMEM = pl.BlockSpec(memory_space=pltpu.VMEM)
 SMEM = pl.BlockSpec(memory_space=pltpu.SMEM)
 PARAMS = pltpu.CompilerParams(vmem_limit_bytes=40 << 20)
@@ -30,7 +32,7 @@
         for which, held in enumerate((own, sib)):
 
             def one(slot, which=which, held=held):
-                r, c = ids[which, 0, slot], ids[which, 1, slot]
+                r, c = ids[which, 0, slot], ids[which, 1 if forward else 3, slot]
                 if forward:
                     total[r] += jnp.dot(held[slot], block(c), preferred_element_type=F32)
                 else:
@@ -40,20 +42,15 @@
 
             count = ids[which, 2, 0]
 
-            @pl.loop(0, slots // CHUNK)
-            def _(turn, one=one, count=count):
-                start = turn * CHUNK
-
-                @pl.when(count >= start + CHUNK)
-                def _():
-                    for u in range(CHUNK):
-                        one(start + u)
-
-                @pl.when((count > start) & (count < start + CHUNK))
-                def _():
-                    @pl.loop(start, count)
-                    def _(slot):
-                        one(slot)
+            done = 0
+            for size in SIZES:
+
+                @pl.loop(done // size, count // size)
+                def _(group, one=one, size=size):
+                    for u in range(size):
+                        one(group * size + u)
+
+                done = count // size * size
 
         out[...] = total[...].astype(BF)
 
@@ -79,7 +76,7 @@
         for s in range(2):
             piece = source[:, s * half : (s + 1) * half]
             for c in range(cols):
-                out[s * cols + c] = piece
+                out[c * 2 + s] = piece
 
     return pl.pallas_call(
         kernel,
@@ -120,7 +117,7 @@
             for d in range(aways):
                 for q in range(pairs):
                     for other, ref in enumerate((own, sibling)):
-                        r = ((spot[1] ^ d) * pairs + (spot[2] ^ q)) * 2 + (spot[0] ^ other)
+                        r = ((spot[2] ^ q) * aways + (spot[1] ^ d)) * 2 + (spot[0] ^ other)
                         at = pl.multiple_of(r * share, share)
                         wgrad[pl.ds(at, share), here] = ref[d, q, s].astype(F32)
 
@@ -214,11 +211,16 @@
     core = lax.axis_index("core")
     swap = [(0, 1), (1, 0)]
 
+
+    def entry(chip, core):
+        return (chip % 2 * RING + chip // 2) * 2 + core
+
     ids = jnp.stack(
         [
-            tile_rows[0, 0],
+            entry(tile_rows[0, 0] // 4, tile_rows[0, 0] // 2 % 2) * own_blocks + tile_rows[0, 0] % 2,
+            entry(tile_cols[0, 0] // 2, core) * own_blocks + tile_cols[0, 0] % 2,
+            jnp.broadcast_to(tile_count[0, 0], (slots,)),
             tile_cols[0, 0] + core * col_blocks,
-            jnp.broadcast_to(tile_count[0, 0], (slots,)),
         ]
     )
     ids = jnp.stack([ids, lax.ppermute(ids, "core", swap)])
@@ -226,11 +228,11 @@
     own = own[0, 0]
     sib = lax.ppermute(own, "core", swap)
 
-    stripe = exchange(sent, ("core", *COL))
+    stripe = exchange(sent, COL_ORDER)
     sums = tile_sums(True, ids, own, sib, stripe, row_blocks)
-    parts = exchange(sums.reshape(2 * chips, own_rows, half), ROW)
+    parts = exchange(sums.reshape(2 * chips, own_rows, half), ROW_ORDER)
     act, grad = middle(parts, weight, cotangent)
-    grad = exchange(grad, ROW)
+    grad = exchange(grad, ROW_ORDER)
 
     wgrad = grad[:, own_rows:].astype(F32).sum(0) * float(nodes) ** (-0.5)
     near, *far = (flip(wgrad, "y", d) for d in range(1, RING))

time: 171 us -> 166 us (0.971)
  no operation moved by 1% of the time
where the time goes in v5:
time: 166 us
  blocking collectives  102 us (61%)
  starting transfers between devices  33.4 us (20%)
  waiting for transfers between devices  13.3 us (8%)
  Pallas kernels  12.5 us (8%)
  local copies, waits for them, and re-layouts  2.37 us (1%)
    all_to_all x3, blocking collectives, exchange(): return lax.all_to_all(array, axes, 0, 0, tiled=True)  102 us
    ppermute x9, starting transfers between devices, flip(): return lax.ppermute(array, axis, [(i, i ^ by) for i in range(size)])  24.5 us
    ppermute x9, waiting for transfers between devices, flip(): return lax.ppermute(array, axis, [(i, i ^ by) for i in range(size)])  11.3 us
    pallas_call x2, Pallas kernels, tile_sums(): pl.pallas_call(kernel, in_specs=[SMEM, VMEM, VMEM, VMEM], out_specs=VMEM,...  8.45 us
    all_to_all x1, starting transfers between devices, exchange(): return lax.all_to_all(array, axes, 0, 0, tiled=True)  7.84 us
  transfers between devices with their start and end apart: 13, of which 5 were waited for; matrix products, arithmetic and copies ran while one was open for 0% of the time, Pallas kernels for 4%

profile of v5, /device:TPU:17, one launch (start us, length us, event | category | flops | bytes accessed | tf_op | source)
XLA Modules:
  0.0 165.9 jit_solution(14203868798173304657)
XLA Ops:
  1.3 0.1 pad.14.clone
  1.4 0.7 fusion.2
  2.1 0.1 pad_add_fusion.1
  2.1 0.7 collective-permute-start
  2.8 0.1 fusion.8
  2.9 0.9 copy-done.3
  3.9 0.1 spread.1
  4.0 0.0 collective-permute-done
  4.0 0.0 copy-start
  4.0 0.1 collective-permute-start.1
  4.1 34.5 %all_to_all.20.source = bf16[16,256,256]{2,1,0:T(8,128)(2,1)S(1)} all-to-all(bf16[16,256,256]{2,1,0:T(8,128)(2,1)S(1)} %spread.1), channel_id=1, replica_groups=mesh['x'=4,'zl'=2,'core'=2,'y'=4,'zh'=2] {'zh','y','core'}, dimensions={0} | all-to-all | bytes 4194304 | tf_op jit(solution)/shard_map/all_to_all | solution.py:194
  38.6 0.0 collective-permute-done.1.sib
  38.6 4.3 %forward_tiles.1 = bf16[32,128,256]{2,1,0:T(8,128)(2,1)S(1)} custom-call(s32[2,4,128]{2,1,0:T(4,128)S(1)} %pad_add_fusion.ids, bf16[128,128,128]{2,1,0:T(8,128)(2,1)S(1)} %bitcast.51, bf16[128,128,128]{2,1,0:T(8,128)(2,1)S(1)} %collective-permute-done.1.sib, bf16[16,256,256]{2,1,0:T(8,128)(2,1)S(1)} %all_to_all.20.source), custom_call_target="tpu_custom_call" | custom-call | flops 2147483648 | bytes 16777216 | tf_op jit(solution)/shard_map/forward_tiles/pallas_call | solution.py:57
  42.9 0.0 copy-start.2
  42.9 0.0 copy-start.4
  42.9 31.3 %all_to_all.21.parts = bf16[16,256,256]{2,1,0:T(8,128)(2,1)S(1)} all-to-all(bf16[16,256,256]{2,1,0:T(8,128)(2,1)S(1)} %bitcast.54), channel_id=1, replica_groups=mesh['x'=4,'zl'=2,'core'=2,'y'=4,'zh'=2] {'zl','x','core'}, dimensions={0} | all-to-all | bytes 4194304 | tf_op jit(solution)/shard_map/all_to_all | solution.py:194
  74.2 0.0 copy-done.4
  74.2 1.4 middle.1
  75.6 36.0 %all_to_all.22.source = bf16[16,320,256]{2,1,0:T(8,128)(2,1)S(1)} all-to-all(bf16[16,320,256]{2,1,0:T(8,128)(2,1)S(1)} %get-tuple-element.16), channel_id=1, replica_groups=mesh['x'=4,'zl'=2,'core'=2,'y'=4,'zh'=2] {'zl','x','core'}, dimensions={0} | all-to-all | bytes 5242880 | tf_op jit(solution)/shard_map/all_to_all | solution.py:194
  111.6 0.1 convert_reduce_fusion
  111.7 2.6 %collective-permute-start.4 = (f32[64,256]{1,0:T(8,128)S(1)}, f32[64,256]{1,0:T(8,128)S(1)}, u32[]{:S(2)}, u32[]{:S(2)}) collective-permute-start(f32[64,256]{1,0:T(8,128)S(1)} %broadcast_multiply_fusion), channel_id=1, source_target_pairs={{0,6},{2,4},{4,2},{6,0},{1,7},{3,5},{5,3},{7,1},{8,14},{10,12},{12... | collective-permute-start | bytes 196616 | tf_op jit(solution)/shard_map/ppermute | solution.py:190
  114.3 1.4 collective-permute-start.3
  115.7 0.5 collective-permute-start.2
  116.2 4.2 %backward_tiles.1 = bf16[32,128,256]{2,1,0:T(8,128)(2,1)S(1)} custom-call(s32[2,4,128]{2,1,0:T(4,128)S(1)} %pad_add_fusion.ids, bf16[128,128,128]{2,1,0:T(8,128)(2,1)S(1)} %bitcast.52, bf16[128,128,128]{2,1,0:T(8,128)(2,1)S(1)} %collective-permute-done.1.sib, bf16[16,320,256]{2,1,0:T(8,128)(2,1)S(1)} %all_to_all.22.source), custom_call_target="tpu_custom_call" | custom-call | flops 2147483648 | bytes 16777216 | tf_op jit(solution)/shard_map/backward_tiles/pallas_call | solution.py:57
  120.4 0.0 copy-start.1
  120.4 1.3 copy-done.1
  121.8 0.0 collective-permute-done.4
  121.8 0.0 collective-permute-done.3
  121.8 0.0 collective-permute-done.2
  121.8 7.8 %all-to-all-start.3 = ((bf16[16,256,256]{2,1,0:T(8,128)(2,1)}), bf16[16,256,256]{2,1,0:T(8,128)(2,1)S(1)}, u32[]{:S(2)}, u32[]{:S(2)}) async-start(bf16[16,256,256]{2,1,0:T(8,128)(2,1)} %bitcast.53), calls=%async_computation.3 | async-start | bytes 4194304 | tf_op jit(solution)/shard_map/all_to_all | solution.py:194
  129.6 2.8 %collective-permute-start.5 = (f32[64,256]{1,0:T(8,128)S(1)}, f32[64,256]{1,0:T(8,128)S(1)}, u32[]{:S(2)}, u32[]{:S(2)}) collective-permute-start(f32[64,256]{1,0:T(8,128)S(1)} %add_add_fusion), channel_id=1, source_target_pairs={{0,1},{1,0},{2,3},{3,2},{4,5},{5,4},{6,7},{7,6},{8,9},{9,8},{10,11... | collective-permute-start | bytes 196616 | tf_op jit(solution)/shard_map/ppermute | solution.py:190
  132.4 0.3 collective-permute-start.7
  132.7 0.3 collective-permute-start.6
  133.0 7.5 %collective-permute-done.5 = f32[64,256]{1,0:T(8,128)S(1)} collective-permute-done((f32[64,256]{1,0:T(8,128)S(1)}, f32[64,256]{1,0:T(8,128)S(1)}, u32[]{:S(2)}, u32[]{:S(2)}) %collective-permute-start.5) | collective-permute-done | bytes 65568 | tf_op jit(solution)/shard_map/ppermute | solution.py:190
  140.5 2.0 %collective-permute-done.7 = f32[64,256]{1,0:T(8,128)S(1)} collective-permute-done((f32[64,256]{1,0:T(8,128)S(1)}, f32[64,256]{1,0:T(8,128)S(1)}, u32[]{:S(2)}, u32[]{:S(2)}) %collective-permute-start.7) | collective-permute-done | bytes 65568 | tf_op jit(solution)/shard_map/ppermute | solution.py:242
  142.5 0.0 collective-permute-done.6
  142.6 0.2 collective-permute-start.10
  142.8 0.6 collective-permute-start.9
  143.4 2.5 %collective-permute-start.8 = (bf16[2,2,32,256]{3,2,1,0:T(8,128)(2,1)S(1)}, bf16[2,2,32,256]{3,2,1,0:T(8,128)(2,1)S(1)}, u32[]{:S(2)}, u32[]{:S(2)}) collective-permute-start(bf16[2,2,32,256]{3,2,1,0:T(8,128)(2,1)S(1)} %pad_maximum_fusion.1), channel_id=1, source_target_pairs={{0,32},{32,0},{64,96},{96,64},{1,33},{33,1},{65,97},{97,65},{2,34}... | collective-permute-start | bytes 196616 | tf_op jit(solution)/shard_map/ppermute | solution.py:190
  145.9 2.1 %collective-permute-done.10 = bf16[2,2,32,256]{3,2,1,0:T(8,128)(2,1)S(1)} collective-permute-done((bf16[2,2,32,256]{3,2,1,0:T(8,128)(2,1)S(1)}, bf16[2,2,32,256]{3,2,1,0:T(8,128)(2,1)S(1)}, u32[]{:S(2)}, u32[]{:S(2)}) %collective-permute-start.10) | collective-permute-done | bytes 65568 | tf_op jit(solution)/shard_map/ppermute | solution.py:190
  148.0 0.0 collective-permute-done.9
  148.0 0.6 collective-permute-done.8
  148.6 13.6 %collective-permute-start.11 = (bf16[4,2,2,32,256]{4,3,2,1,0:T(8,128)(2,1)S(1)}, bf16[4,2,2,32,256]{4,3,2,1,0:T(8,128)(2,1)S(1)}, u32[]{:S(2)}, u32[]{:S(2)}) collective-permute-start(bf16[4,2,2,32,256]{4,3,2,1,0:T(8,128)(2,1)S(1)} %pad_maximum_fusion.own), channel_id=1, source_target_pairs={{0,8},{8,0},{1,9},{9,1},{2,10},{10,2},{3,11},{11,3},{4,12},{12,4},... | collective-permute-start | bytes 786440 | tf_op jit(solution)/shard_map/ppermute | solution.py:190
  162.2 0.1 pad_add_fusion.2.spot
  162.3 1.1 collective-permute-done.11.sibling
  163.4 1.6 place_shares.1
  165.0 0.0 all-to-all-done.3.parts
  165.0 1.0 column_sum.1
  (10 shorter events, 0.1 us)
Async XLA Ops:
  2.1 1.9 %collective-permute-start = (s32[4,128]{1,0:T(4,128)S(1)}, s32[4,128]{1,0:T(4,128)S(1)}, u32[]{:S(2)}, u32[]{:S(2)}) collective-permute-start(s32[4,128]{1,0:T(4,128)S(1)} %pad_add_fusion.1), channel_id=1, source_target_pairs={{0,8},{8,0},{1,9},{9,1},{2,10},{10,2},{3,11},{11,3},{4,12},{12,4},... | collective-permute-start | bytes 6152 | tf_op jit(solution)/shard_map/ppermute | solution.py:226
  2.9 0.9 copy-start.3
  4.0 34.6 %copy-start = (bf16[1,1,128,128,128]{4,3,2,1,0:T(8,128)(2,1)S(1)}, bf16[1,1,128,128,128]{4,3,2,1,0:T(8,128)(2,1)}, u32[]{:S(2)}) copy-start(bf16[1,1,128,128,128]{4,3,2,1,0:T(8,128)(2,1)} %param.10) | copy-start | bytes 12582916
  4.0 34.6 %collective-permute-start.1 = (bf16[128,128,128]{2,1,0:T(8,128)(2,1)}, bf16[128,128,128]{2,1,0:T(8,128)(2,1)S(1)}, u32[]{:S(2)}, u32[]{:S(2)}) collective-permute-start(bf16[128,128,128]{2,1,0:T(8,128)(2,1)} %bitcast.50), channel_id=1, source_target_pairs={{0,8},{8,0},{1,9},{9,1},{2,10},{10,2},{3,11},{11,3},{4,12},{12,4},... | collective-permute-start | bytes 12582920 | tf_op jit(solution)/shard_map/ppermute | solution.py:229
  42.9 31.4 %copy-start.2 = (bf16[512,512]{1,0:T(8,128)(2,1)S(1)}, bf16[512,512]{1,0:T(8,128)(2,1)}, u32[]{:S(2)}) copy-start(bf16[512,512]{1,0:T(8,128)(2,1)} %weight.1) | copy-start | bytes 1572868
  42.9 31.4 %copy-start.4 = (bf16[256,512]{1,0:T(8,128)(2,1)S(1)}, bf16[256,512]{1,0:T(8,128)(2,1)}, u32[]{:S(2)}) copy-start(bf16[256,512]{1,0:T(8,128)(2,1)} %cot.1) | copy-start | bytes 786436
  111.7 10.0 %collective-permute-start.4 = (f32[64,256]{1,0:T(8,128)S(1)}, f32[64,256]{1,0:T(8,128)S(1)}, u32[]{:S(2)}, u32[]{:S(2)}) collective-permute-start(f32[64,256]{1,0:T(8,128)S(1)} %broadcast_multiply_fusion), channel_id=1, source_target_pairs={{0,6},{2,4},{4,2},{6,0},{1,7},{3,5},{5,3},{7,1},{8,14},{10,12},{12... | collective-permute-start | bytes 196616 | tf_op jit(solution)/shard_map/ppermute | solution.py:190
  114.3 7.4 %collective-permute-start.3 = (f32[64,256]{1,0:T(8,128)S(1)}, f32[64,256]{1,0:T(8,128)S(1)}, u32[]{:S(2)}, u32[]{:S(2)}) collective-permute-start(f32[64,256]{1,0:T(8,128)S(1)} %broadcast_multiply_fusion), channel_id=1, source_target_pairs={{0,4},{2,6},{4,0},{6,2},{1,5},{3,7},{5,1},{7,3},{8,12},{10,14},{12... | collective-permute-start | bytes 196616 | tf_op jit(solution)/shard_map/ppermute | solution.py:190
  115.7 6.1 %collective-permute-start.2 = (f32[64,256]{1,0:T(8,128)S(1)}, f32[64,256]{1,0:T(8,128)S(1)}, u32[]{:S(2)}, u32[]{:S(2)}) collective-permute-start(f32[64,256]{1,0:T(8,128)S(1)} %broadcast_multiply_fusion), channel_id=1, source_target_pairs={{0,2},{2,0},{4,6},{6,4},{1,3},{3,1},{5,7},{7,5},{8,10},{10,8},{12,... | collective-permute-start | bytes 196616 | tf_op jit(solution)/shard_map/ppermute | solution.py:190
  120.4 1.3 copy-start.1
  121.8 43.2 %all-to-all-start.3 = ((bf16[16,256,256]{2,1,0:T(8,128)(2,1)}), bf16[16,256,256]{2,1,0:T(8,128)(2,1)S(1)}, u32[]{:S(2)}, u32[]{:S(2)}) async-start(bf16[16,256,256]{2,1,0:T(8,128)(2,1)} %bitcast.53), calls=%async_computation.3 | async-start | bytes 4194304 | tf_op jit(solution)/shard_map/all_to_all | solution.py:194
  129.6 10.9 %collective-permute-start.5 = (f32[64,256]{1,0:T(8,128)S(1)}, f32[64,256]{1,0:T(8,128)S(1)}, u32[]{:S(2)}, u32[]{:S(2)}) collective-permute-start(f32[64,256]{1,0:T(8,128)S(1)} %add_add_fusion), channel_id=1, source_target_pairs={{0,1},{1,0},{2,3},{3,2},{4,5},{5,4},{6,7},{7,6},{8,9},{9,8},{10,11... | collective-permute-start | bytes 196616 | tf_op jit(solution)/shard_map/ppermute | solution.py:190
  132.4 10.1 %collective-permute-start.7 = (f32[64,256]{1,0:T(8,128)S(1)}, f32[64,256]{1,0:T(8,128)S(1)}, u32[]{:S(2)}, u32[]{:S(2)}) collective-permute-start(f32[64,256]{1,0:T(8,128)S(1)} %add_add_fusion), channel_id=1, source_target_pairs={{0,17},{1,16},{16,1},{17,0},{2,19},{3,18},{18,3},{19,2},{4,21},{5,... | collective-permute-start | bytes 196616 | tf_op jit(solution)/shard_map/ppermute | solution.py:242
  132.7 9.9 %collective-permute-start.6 = (f32[64,256]{1,0:T(8,128)S(1)}, f32[64,256]{1,0:T(8,128)S(1)}, u32[]{:S(2)}, u32[]{:S(2)}) collective-permute-start(f32[64,256]{1,0:T(8,128)S(1)} %add_add_fusion), channel_id=1, source_target_pairs={{0,16},{16,0},{1,17},{17,1},{2,18},{18,2},{3,19},{19,3},{4,20},{20... | collective-permute-start | bytes 196616 | tf_op jit(solution)/shard_map/ppermute | solution.py:190
  142.6 5.4 %collective-permute-start.10 = (bf16[2,2,32,256]{3,2,1,0:T(8,128)(2,1)S(1)}, bf16[2,2,32,256]{3,2,1,0:T(8,128)(2,1)S(1)}, u32[]{:S(2)}, u32[]{:S(2)}) collective-permute-start(bf16[2,2,32,256]{3,2,1,0:T(8,128)(2,1)S(1)} %pad_maximum_fusion.1), channel_id=1, source_target_pairs={{0,96},{32,64},{64,32},{96,0},{1,97},{33,65},{65,33},{97,1},{2,98}... | collective-permute-start | bytes 196616 | tf_op jit(solution)/shard_map/ppermute | solution.py:190
  142.8 5.2 %collective-permute-start.9 = (bf16[2,2,32,256]{3,2,1,0:T(8,128)(2,1)S(1)}, bf16[2,2,32,256]{3,2,1,0:T(8,128)(2,1)S(1)}, u32[]{:S(2)}, u32[]{:S(2)}) collective-permute-start(bf16[2,2,32,256]{3,2,1,0:T(8,128)(2,1)S(1)} %pad_maximum_fusion.1), channel_id=1, source_target_pairs={{0,64},{32,96},{64,0},{96,32},{1,65},{33,97},{65,1},{97,33},{2,66}... | collective-permute-start | bytes 196616 | tf_op jit(solution)/shard_map/ppermute | solution.py:190
  143.4 5.2 %collective-permute-start.8 = (bf16[2,2,32,256]{3,2,1,0:T(8,128)(2,1)S(1)}, bf16[2,2,32,256]{3,2,1,0:T(8,128)(2,1)S(1)}, u32[]{:S(2)}, u32[]{:S(2)}) collective-permute-start(bf16[2,2,32,256]{3,2,1,0:T(8,128)(2,1)S(1)} %pad_maximum_fusion.1), channel_id=1, source_target_pairs={{0,32},{32,0},{64,96},{96,64},{1,33},{33,1},{65,97},{97,65},{2,34}... | collective-permute-start | bytes 196616 | tf_op jit(solution)/shard_map/ppermute | solution.py:190
  148.6 14.8 %collective-permute-start.11 = (bf16[4,2,2,32,256]{4,3,2,1,0:T(8,128)(2,1)S(1)}, bf16[4,2,2,32,256]{4,3,2,1,0:T(8,128)(2,1)S(1)}, u32[]{:S(2)}, u32[]{:S(2)}) collective-permute-start(bf16[4,2,2,32,256]{4,3,2,1,0:T(8,128)(2,1)S(1)} %pad_maximum_fusion.own), channel_id=1, source_target_pairs={{0,8},{8,0},{1,9},{9,1},{2,10},{10,2},{3,11},{11,3},{4,12},{12,4},... | collective-permute-start | bytes 786440 | tf_op jit(solution)/shard_map/ppermute | solution.py:190

commit v6 on v5

--- a/solution.py
+++ b/solution.py
@@ -7,7 +7,7 @@
 
 BF = jnp.bfloat16
 F32 = jnp.float32
-SIZES = (64, 16, 1)
+SIZES = (64, 32, 8, 1)
 RING = 4
 ROW = ("x", "zl", "core")
 COL = ("y", "zh")

time: 166 us -> 167 us (level)
  no operation moved by 1% of the time
where the time goes in v6:
time: 167 us; the launch traced here: 166 us
  blocking collectives  101 us (60%)
  starting transfers between devices  33.6 us (20%)
  waiting for transfers between devices  13.9 us (8%)
  Pallas kernels  13.4 us (8%)
  local copies, waits for them, and re-layouts  2.37 us (1%)
    all_to_all x3, blocking collectives, exchange(): return lax.all_to_all(array, axes, 0, 0, tiled=True)  101 us
    ppermute x9, starting transfers between devices, flip(): return lax.ppermute(array, axis, [(i, i ^ by) for i in range(size)])  24.7 us
    ppermute x9, waiting for transfers between devices, flip(): return lax.ppermute(array, axis, [(i, i ^ by) for i in range(size)])  11.8 us
    pallas_call x2, Pallas kernels, tile_sums(): pl.pallas_call(kernel, in_specs=[SMEM, VMEM, VMEM, VMEM], out_specs=VMEM,...  9.27 us
    all_to_all x1, starting transfers between devices, exchange(): return lax.all_to_all(array, axes, 0, 0, tiled=True)  8.13 us
  transfers between devices with their start and end apart: 13, of which 5 were waited for; matrix products, arithmetic and copies ran while one was open for 0% of the time, Pallas kernels for 4%

profile of v6, /device:TPU:17, one launch (start us, length us, event | category | flops | bytes accessed | tf_op | source)
XLA Modules:
  0.0 166.4 jit_solution(13593614814427062925)
XLA Ops:
  1.3 0.1 pad.14.clone
  1.4 0.7 fusion.2
  2.1 0.1 pad_add_fusion.1
  2.1 0.7 collective-permute-start
  2.8 0.1 fusion.8
  2.9 0.9 copy-done.3
  3.9 0.1 spread.1
  4.0 0.0 collective-permute-done
  4.0 0.0 copy-start
  4.0 0.1 collective-permute-start.1
  4.1 34.5 %all_to_all.20.source = bf16[16,256,256]{2,1,0:T(8,128)(2,1)S(1)} all-to-all(bf16[16,256,256]{2,1,0:T(8,128)(2,1)S(1)} %spread.1), channel_id=1, replica_groups=mesh['x'=4,'zl'=2,'core'=2,'y'=4,'zh'=2] {'zh','y','core'}, dimensions={0} | all-to-all | bytes 4194304 | tf_op jit(solution)/shard_map/all_to_all | solution.py:194
  38.6 0.0 collective-permute-done.1.sib
  38.6 0.0 copy-done
  38.6 4.6 %forward_tiles.1 = bf16[32,128,256]{2,1,0:T(8,128)(2,1)S(1)} custom-call(s32[2,4,128]{2,1,0:T(4,128)S(1)} %pad_add_fusion.ids, bf16[128,128,128]{2,1,0:T(8,128)(2,1)S(1)} %bitcast.51, bf16[128,128,128]{2,1,0:T(8,128)(2,1)S(1)} %collective-permute-done.1.sib, bf16[16,256,256]{2,1,0:T(8,128)(2,1)S(1)} %all_to_all.20.source), custom_call_target="tpu_custom_call" | custom-call | flops 2147483648 | bytes 16777216 | tf_op jit(solution)/shard_map/forward_tiles/pallas_call | solution.py:57
  43.2 0.0 copy-start.2
  43.2 0.0 copy-start.4
  43.2 30.2 %all_to_all.21.parts = bf16[16,256,256]{2,1,0:T(8,128)(2,1)S(1)} all-to-all(bf16[16,256,256]{2,1,0:T(8,128)(2,1)S(1)} %bitcast.54), channel_id=1, replica_groups=mesh['x'=4,'zl'=2,'core'=2,'y'=4,'zh'=2] {'zl','x','core'}, dimensions={0} | all-to-all | bytes 4194304 | tf_op jit(solution)/shard_map/all_to_all | solution.py:194
  73.4 0.0 copy-done.4
  73.4 1.4 middle.1
  74.8 36.0 %all_to_all.22.source = bf16[16,320,256]{2,1,0:T(8,128)(2,1)S(1)} all-to-all(bf16[16,320,256]{2,1,0:T(8,128)(2,1)S(1)} %get-tuple-element.16), channel_id=1, replica_groups=mesh['x'=4,'zl'=2,'core'=2,'y'=4,'zh'=2] {'zl','x','core'}, dimensions={0} | all-to-all | bytes 5242880 | tf_op jit(solution)/shard_map/all_to_all | solution.py:194
  110.8 0.1 convert_reduce_fusion
  110.9 1.6 collective-permute-start.4
  112.5 3.2 %collective-permute-start.3 = (f32[64,256]{1,0:T(8,128)S(1)}, f32[64,256]{1,0:T(8,128)S(1)}, u32[]{:S(2)}, u32[]{:S(2)}) collective-permute-start(f32[64,256]{1,0:T(8,128)S(1)} %broadcast_multiply_fusion), channel_id=1, source_target_pairs={{0,4},{2,6},{4,0},{6,2},{1,5},{3,7},{5,1},{7,3},{8,12},{10,14},{12... | collective-permute-start | bytes 196616 | tf_op jit(solution)/shard_map/ppermute | solution.py:190
  115.8 0.8 collective-permute-start.2
  116.6 4.7 %backward_tiles.1 = bf16[32,128,256]{2,1,0:T(8,128)(2,1)S(1)} custom-call(s32[2,4,128]{2,1,0:T(4,128)S(1)} %pad_add_fusion.ids, bf16[128,128,128]{2,1,0:T(8,128)(2,1)S(1)} %bitcast.52, bf16[128,128,128]{2,1,0:T(8,128)(2,1)S(1)} %collective-permute-done.1.sib, bf16[16,320,256]{2,1,0:T(8,128)(2,1)S(1)} %all_to_all.22.source), custom_call_target="tpu_custom_call" | custom-call | flops 2147483648 | bytes 16777216 | tf_op jit(solution)/shard_map/backward_tiles/pallas_call | solution.py:57
  121.3 1.3 copy-done.1
  122.6 0.0 collective-permute-done.4
  122.6 0.0 collective-permute-done.3
  122.6 0.0 collective-permute-done.2
  122.6 8.1 %all-to-all-start.3 = ((bf16[16,256,256]{2,1,0:T(8,128)(2,1)}), bf16[16,256,256]{2,1,0:T(8,128)(2,1)S(1)}, u32[]{:S(2)}, u32[]{:S(2)}) async-start(bf16[16,256,256]{2,1,0:T(8,128)(2,1)} %bitcast.53), calls=%async_computation.3 | async-start | bytes 4194304 | tf_op jit(solution)/shard_map/all_to_all | solution.py:194
  130.7 2.8 %collective-permute-start.5 = (f32[64,256]{1,0:T(8,128)S(1)}, f32[64,256]{1,0:T(8,128)S(1)}, u32[]{:S(2)}, u32[]{:S(2)}) collective-permute-start(f32[64,256]{1,0:T(8,128)S(1)} %add_add_fusion), channel_id=1, source_target_pairs={{0,1},{1,0},{2,3},{3,2},{4,5},{5,4},{6,7},{7,6},{8,9},{9,8},{10,11... | collective-permute-start | bytes 196616 | tf_op jit(solution)/shard_map/ppermute | solution.py:190
  133.5 0.0 collective-permute-start.7
  133.5 0.0 collective-permute-start.6
  133.5 8.1 %collective-permute-done.5 = f32[64,256]{1,0:T(8,128)S(1)} collective-permute-done((f32[64,256]{1,0:T(8,128)S(1)}, f32[64,256]{1,0:T(8,128)S(1)}, u32[]{:S(2)}, u32[]{:S(2)}) %collective-permute-start.5) | collective-permute-done | bytes 65568 | tf_op jit(solution)/shard_map/ppermute | solution.py:190
  141.6 2.1 %collective-permute-done.7 = f32[64,256]{1,0:T(8,128)S(1)} collective-permute-done((f32[64,256]{1,0:T(8,128)S(1)}, f32[64,256]{1,0:T(8,128)S(1)}, u32[]{:S(2)}, u32[]{:S(2)}) %collective-permute-start.7) | collective-permute-done | bytes 65568 | tf_op jit(solution)/shard_map/ppermute | solution.py:242
  143.7 0.0 collective-permute-done.6
  143.7 0.1 collective-permute-start.10
  143.8 0.1 collective-permute-start.9
  143.9 3.1 %collective-permute-start.8 = (bf16[2,2,32,256]{3,2,1,0:T(8,128)(2,1)S(1)}, bf16[2,2,32,256]{3,2,1,0:T(8,128)(2,1)S(1)}, u32[]{:S(2)}, u32[]{:S(2)}) collective-permute-start(bf16[2,2,32,256]{3,2,1,0:T(8,128)(2,1)S(1)} %pad_maximum_fusion.1), channel_id=1, source_target_pairs={{0,32},{32,0},{64,96},{96,64},{1,33},{33,1},{65,97},{97,65},{2,34}... | collective-permute-start | bytes 196616 | tf_op jit(solution)/shard_map/ppermute | solution.py:190
  147.0 2.1 %collective-permute-done.10 = bf16[2,2,32,256]{3,2,1,0:T(8,128)(2,1)S(1)} collective-permute-done((bf16[2,2,32,256]{3,2,1,0:T(8,128)(2,1)S(1)}, bf16[2,2,32,256]{3,2,1,0:T(8,128)(2,1)S(1)}, u32[]{:S(2)}, u32[]{:S(2)}) %collective-permute-start.10) | collective-permute-done | bytes 65568 | tf_op jit(solution)/shard_map/ppermute | solution.py:190
  149.1 0.0 collective-permute-done.9
  149.1 0.6 collective-permute-done.8
  149.7 13.0 %collective-permute-start.11 = (bf16[4,2,2,32,256]{4,3,2,1,0:T(8,128)(2,1)S(1)}, bf16[4,2,2,32,256]{4,3,2,1,0:T(8,128)(2,1)S(1)}, u32[]{:S(2)}, u32[]{:S(2)}) collective-permute-start(bf16[4,2,2,32,256]{4,3,2,1,0:T(8,128)(2,1)S(1)} %pad_maximum_fusion.own), channel_id=1, source_target_pairs={{0,8},{8,0},{1,9},{9,1},{2,10},{10,2},{3,11},{11,3},{4,12},{12,4},... | collective-permute-start | bytes 786440 | tf_op jit(solution)/shard_map/ppermute | solution.py:190
  162.7 0.1 pad_add_fusion.2.spot
  162.7 1.1 collective-permute-done.11.sibling
  163.8 1.6 place_shares.1
  165.4 0.0 all-to-all-done.3.parts
  165.4 1.0 column_sum.1
  (10 shorter events, 0.1 us)
Async XLA Ops:
  2.1 1.9 %collective-permute-start = (s32[4,128]{1,0:T(4,128)S(1)}, s32[4,128]{1,0:T(4,128)S(1)}, u32[]{:S(2)}, u32[]{:S(2)}) collective-permute-start(s32[4,128]{1,0:T(4,128)S(1)} %pad_add_fusion.1), channel_id=1, source_target_pairs={{0,8},{8,0},{1,9},{9,1},{2,10},{10,2},{3,11},{11,3},{4,12},{12,4},... | collective-permute-start | bytes 6152 | tf_op jit(solution)/shard_map/ppermute | solution.py:226
  2.9 0.9 copy-start.3
  4.0 34.6 %copy-start = (bf16[1,1,128,128,128]{4,3,2,1,0:T(8,128)(2,1)S(1)}, bf16[1,1,128,128,128]{4,3,2,1,0:T(8,128)(2,1)}, u32[]{:S(2)}) copy-start(bf16[1,1,128,128,128]{4,3,2,1,0:T(8,128)(2,1)} %param.10) | copy-start | bytes 12582916
  4.0 34.6 %collective-permute-start.1 = (bf16[128,128,128]{2,1,0:T(8,128)(2,1)}, bf16[128,128,128]{2,1,0:T(8,128)(2,1)S(1)}, u32[]{:S(2)}, u32[]{:S(2)}) collective-permute-start(bf16[128,128,128]{2,1,0:T(8,128)(2,1)} %bitcast.50), channel_id=1, source_target_pairs={{0,8},{8,0},{1,9},{9,1},{2,10},{10,2},{3,11},{11,3},{4,12},{12,4},... | collective-permute-start | bytes 12582920 | tf_op jit(solution)/shard_map/ppermute | solution.py:229
  43.2 30.2 %copy-start.2 = (bf16[512,512]{1,0:T(8,128)(2,1)S(1)}, bf16[512,512]{1,0:T(8,128)(2,1)}, u32[]{:S(2)}) copy-start(bf16[512,512]{1,0:T(8,128)(2,1)} %weight.1) | copy-start | bytes 1572868
  43.2 30.2 %copy-start.4 = (bf16[256,512]{1,0:T(8,128)(2,1)S(1)}, bf16[256,512]{1,0:T(8,128)(2,1)}, u32[]{:S(2)}) copy-start(bf16[256,512]{1,0:T(8,128)(2,1)} %cot.1) | copy-start | bytes 786436
  110.9 11.7 %collective-permute-start.4 = (f32[64,256]{1,0:T(8,128)S(1)}, f32[64,256]{1,0:T(8,128)S(1)}, u32[]{:S(2)}, u32[]{:S(2)}) collective-permute-start(f32[64,256]{1,0:T(8,128)S(1)} %broadcast_multiply_fusion), channel_id=1, source_target_pairs={{0,6},{2,4},{4,2},{6,0},{1,7},{3,5},{5,3},{7,1},{8,14},{10,12},{12... | collective-permute-start | bytes 196616 | tf_op jit(solution)/shard_map/ppermute | solution.py:190
  112.5 10.1 %collective-permute-start.3 = (f32[64,256]{1,0:T(8,128)S(1)}, f32[64,256]{1,0:T(8,128)S(1)}, u32[]{:S(2)}, u32[]{:S(2)}) collective-permute-start(f32[64,256]{1,0:T(8,128)S(1)} %broadcast_multiply_fusion), channel_id=1, source_target_pairs={{0,4},{2,6},{4,0},{6,2},{1,5},{3,7},{5,1},{7,3},{8,12},{10,14},{12... | collective-permute-start | bytes 196616 | tf_op jit(solution)/shard_map/ppermute | solution.py:190
  115.8 6.8 %collective-permute-start.2 = (f32[64,256]{1,0:T(8,128)S(1)}, f32[64,256]{1,0:T(8,128)S(1)}, u32[]{:S(2)}, u32[]{:S(2)}) collective-permute-start(f32[64,256]{1,0:T(8,128)S(1)} %broadcast_multiply_fusion), channel_id=1, source_target_pairs={{0,2},{2,0},{4,6},{6,4},{1,3},{3,1},{5,7},{7,5},{8,10},{10,8},{12,... | collective-permute-start | bytes 196616 | tf_op jit(solution)/shard_map/ppermute | solution.py:190
  121.2 1.3 copy-start.1
  122.6 42.8 %all-to-all-start.3 = ((bf16[16,256,256]{2,1,0:T(8,128)(2,1)}), bf16[16,256,256]{2,1,0:T(8,128)(2,1)S(1)}, u32[]{:S(2)}, u32[]{:S(2)}) async-start(bf16[16,256,256]{2,1,0:T(8,128)(2,1)} %bitcast.53), calls=%async_computation.3 | async-start | bytes 4194304 | tf_op jit(solution)/shard_map/all_to_all | solution.py:194
  130.7 10.8 %collective-permute-start.5 = (f32[64,256]{1,0:T(8,128)S(1)}, f32[64,256]{1,0:T(8,128)S(1)}, u32[]{:S(2)}, u32[]{:S(2)}) collective-permute-start(f32[64,256]{1,0:T(8,128)S(1)} %add_add_fusion), channel_id=1, source_target_pairs={{0,1},{1,0},{2,3},{3,2},{4,5},{5,4},{6,7},{7,6},{8,9},{9,8},{10,11... | collective-permute-start | bytes 196616 | tf_op jit(solution)/shard_map/ppermute | solution.py:190
  133.5 10.1 %collective-permute-start.7 = (f32[64,256]{1,0:T(8,128)S(1)}, f32[64,256]{1,0:T(8,128)S(1)}, u32[]{:S(2)}, u32[]{:S(2)}) collective-permute-start(f32[64,256]{1,0:T(8,128)S(1)} %add_add_fusion), channel_id=1, source_target_pairs={{0,17},{1,16},{16,1},{17,0},{2,19},{3,18},{18,3},{19,2},{4,21},{5,... | collective-permute-start | bytes 196616 | tf_op jit(solution)/shard_map/ppermute | solution.py:242
  133.5 10.1 %collective-permute-start.6 = (f32[64,256]{1,0:T(8,128)S(1)}, f32[64,256]{1,0:T(8,128)S(1)}, u32[]{:S(2)}, u32[]{:S(2)}) collective-permute-start(f32[64,256]{1,0:T(8,128)S(1)} %add_add_fusion), channel_id=1, source_target_pairs={{0,16},{16,0},{1,17},{17,1},{2,18},{18,2},{3,19},{19,3},{4,20},{20... | collective-permute-start | bytes 196616 | tf_op jit(solution)/shard_map/ppermute | solution.py:190
  143.7 5.4 %collective-permute-start.10 = (bf16[2,2,32,256]{3,2,1,0:T(8,128)(2,1)S(1)}, bf16[2,2,32,256]{3,2,1,0:T(8,128)(2,1)S(1)}, u32[]{:S(2)}, u32[]{:S(2)}) collective-permute-start(bf16[2,2,32,256]{3,2,1,0:T(8,128)(2,1)S(1)} %pad_maximum_fusion.1), channel_id=1, source_target_pairs={{0,96},{32,64},{64,32},{96,0},{1,97},{33,65},{65,33},{97,1},{2,98}... | collective-permute-start | bytes 196616 | tf_op jit(solution)/shard_map/ppermute | solution.py:190
  143.8 5.3 %collective-permute-start.9 = (bf16[2,2,32,256]{3,2,1,0:T(8,128)(2,1)S(1)}, bf16[2,2,32,256]{3,2,1,0:T(8,128)(2,1)S(1)}, u32[]{:S(2)}, u32[]{:S(2)}) collective-permute-start(bf16[2,2,32,256]{3,2,1,0:T(8,128)(2,1)S(1)} %pad_maximum_fusion.1), channel_id=1, source_target_pairs={{0,64},{32,96},{64,0},{96,32},{1,65},{33,97},{65,1},{97,33},{2,66}... | collective-permute-start | bytes 196616 | tf_op jit(solution)/shard_map/ppermute | solution.py:190
  143.9 5.8 %collective-permute-start.8 = (bf16[2,2,32,256]{3,2,1,0:T(8,128)(2,1)S(1)}, bf16[2,2,32,256]{3,2,1,0:T(8,128)(2,1)S(1)}, u32[]{:S(2)}, u32[]{:S(2)}) collective-permute-start(bf16[2,2,32,256]{3,2,1,0:T(8,128)(2,1)S(1)} %pad_maximum_fusion.1), channel_id=1, source_target_pairs={{0,32},{32,0},{64,96},{96,64},{1,33},{33,1},{65,97},{97,65},{2,34}... | collective-permute-start | bytes 196616 | tf_op jit(solution)/shard_map/ppermute | solution.py:190
  149.7 14.1 %collective-permute-start.11 = (bf16[4,2,2,32,256]{4,3,2,1,0:T(8,128)(2,1)S(1)}, bf16[4,2,2,32,256]{4,3,2,1,0:T(8,128)(2,1)S(1)}, u32[]{:S(2)}, u32[]{:S(2)}) collective-permute-start(bf16[4,2,2,32,256]{4,3,2,1,0:T(8,128)(2,1)S(1)} %pad_maximum_fusion.own), channel_id=1, source_target_pairs={{0,8},{8,0},{1,9},{9,1},{2,10},{10,2},{3,11},{11,3},{4,12},{12,4},... | collective-permute-start | bytes 786440 | tf_op jit(solution)/shard_map/ppermute | solution.py:190
